TPU v7x, 32 devices: a whole 2x2x4 slice. The times are simulated.
32 devices in a mesh: gx: 8 (over y, x, core), ao: 4 (over z).
Axes of the slice: x: 2, y: 2, z: 4, core: 2. Of those that a mesh axis runs over, the one named last changes fastest.
Arguments:
- density: bfloat16 [384, 128, 1024], P('ao', 'gx'), may hold values from 0 to 2
- kernel: bfloat16 [384, 384], replicated, may hold values from -0.0102062073 to 0.0102062073
- neighbours: int32 [384, 6], replicated, may hold values from 0 to 383, as said below
- weights: int32 [384, 6], replicated, may hold values from 1 to 3
- signs: int32 [2, 384], replicated, may hold values from 0 to 1
- speeds: float32 [2, 384], replicated, may hold values from 0.05 to 0.2
Outputs:
- evolved: bfloat16 [384, 128, 1024], P('ao', 'gx')
Inputs may be any that keep to these rules, and one draw needn't show every extreme that they name: `neighbours`: each entry names an orientation other than its own row's.
All inputs are finite; a program needn't handle non-finite values.
Results may differ from a plain program's by a relative error of at most 0.0052.
Values may be sent and summed in bfloat16 or wider, within the bound.
No kernel may reach another device: no remote copies, remote signals or barrier semaphores. Data moves between devices by JAX's collectives and lax.ppermute only.
A program may use at most 128 MiB of HBM per device.

v0:
```python
import functools

import jax
import jax.numpy as jnp
from jax import lax
from jax.experimental import pallas as pl
from jax.experimental.pallas import tpu as pltpu
from jax.sharding import PartitionSpec as P

TIME_STEPS = 3


rotation_rate = 0.05


def extended(value, sides, width):
    for axis, dim in sides:
        devices, length = (lax.axis_size(axis), value.shape[dim])
        up = [(i, (i + 1) % devices) for i in range(devices)]
        down = [(j, i) for i, j in up]
        last = lax.slice_in_dim(value, length - width, length, axis=dim)
        leading = lax.slice_in_dim(value, 0, width, axis=dim)
        before = lax.ppermute(last, axis, up)
        after = lax.ppermute(leading, axis, down)
        value = jnp.concatenate([before, value, after], axis=dim)
    return value


def upwind(centre, behind_one, behind_two, ahead_one, ahead_two, direction, speed):
    rear = 0.5 * (3.0 * centre - 4.0 * behind_one + behind_two)
    front = 0.5 * (3.0 * centre - 4.0 * ahead_one + ahead_two)
    return speed * jnp.where(direction == 1, rear, front)


def stencil_matrix(neighbours, weights):
    number = neighbours.shape[0]
    labels = jnp.arange(number, dtype=jnp.int32)
    matches = (neighbours[:, :, None] == labels[None, None, :]).astype(jnp.float32)
    scaled = weights.astype(jnp.float32)
    coupled = jnp.sum(scaled[:, :, None] * matches, axis=1)
    totals = jnp.sum(scaled, axis=1)
    identity = (labels[:, None] == labels[None, :]).astype(jnp.float32)
    return (coupled - totals[:, None] * identity).astype(jnp.bfloat16)


def rotate_block(block, kernel, turn_matrix):
    block_shape = block.shape
    values = block.reshape(block_shape[0], -1)
    potential = jnp.dot(kernel, values, preferred_element_type=jnp.float32)
    wide_values = values.astype(jnp.float32)
    drifted = (wide_values * (1.0 + potential)).astype(jnp.bfloat16)
    turned = jnp.dot(turn_matrix, drifted, preferred_element_type=jnp.float32)
    return (wide_values + rotation_rate * turned).astype(jnp.bfloat16).reshape(block_shape)


def per_device(density, kernel, neighbours, weights, signs, speeds):
    turn_matrix = stencil_matrix(neighbours, weights)
    share = density.shape[0]
    offset = lax.axis_index("ao") * share
    local_signs = lax.dynamic_slice_in_dim(signs, offset, share, 1)
    local_speeds = lax.dynamic_slice_in_dim(speeds, offset, share, 1)
    current = density
    for section_index in range(TIME_STEPS):
        widened = extended(current, (("gx", 1),), 2).astype(jnp.float32)
        centre = current.astype(jnp.float32)
        along_rows = upwind(
            centre,
            widened[:, 1:-3],
            widened[:, :-4],
            widened[:, 3:-1],
            widened[:, 4:],
            local_signs[0][:, None, None],
            local_speeds[0][:, None, None],
        )
        along_columns = upwind(
            centre,
            jnp.roll(centre, 1, 2),
            jnp.roll(centre, 2, 2),
            jnp.roll(centre, -1, 2),
            jnp.roll(centre, -2, 2),
            local_signs[1][:, None, None],
            local_speeds[1][:, None, None],
        )
        advected = (centre - along_rows - along_columns).astype(jnp.bfloat16)
        current = lax.all_to_all(
            rotate_block(
                lax.all_to_all(advected, "ao", split_axis=2, concat_axis=0, tiled=True),
                kernel,
                turn_matrix,
            ),
            "ao",
            split_axis=0,
            concat_axis=2,
            tiled=True,
        )
    return current


LANES = 128
REACH = 2 * TIME_STEPS
GROUP = 8
SLOT = LANES // GROUP


def pack_kernel(place, main_ref, before_ref, after_ref, out_ref, main, sides):
    orients, rows, _ = main_ref.shape
    lane = lax.broadcasted_iota(jnp.int32, (orients, LANES), 1)
    main[...] = main_ref[...].astype(jnp.float32).reshape(orients * rows, LANES)
    wide_lane = lax.broadcasted_iota(jnp.int32, (orients * rows, LANES), 1)
    sides[...] = jnp.where(
        wide_lane < LANES // 2,
        after_ref[...].astype(jnp.float32).reshape(orients * rows, LANES),
        before_ref[...].astype(jnp.float32).reshape(orients * rows, LANES),
    )
    owner = ((lane + SLOT // 2) % LANES) // SLOT
    for group in range(rows // GROUP):
        packed = jnp.zeros((orients, LANES), jnp.float32)
        for slot in range(GROUP):
            row = group * GROUP + slot
            out_ref[1 + row] = main[pl.ds(row, orients, stride=rows), :].astype(jnp.bfloat16)
            edge = pltpu.roll(sides[pl.ds(row, orients, stride=rows), :], SLOT * slot, 1)
            packed = jnp.where(owner == slot, edge, packed)
        out_ref[0 if group == 0 else rows + 1] = packed.astype(jnp.bfloat16)


def pack(density, place, shift, part, devices, parts):
    share, rows, columns = density.shape
    tiles = columns // LANES
    step = share

    def tile(offset):
        def index(block, place_ref):
            target = lax.rem(place_ref[0] + shift, devices)
            return block, 0, lax.rem(target * parts + part + offset + tiles, tiles)

        return pl.BlockSpec((step, rows, LANES), index)

    return pl.pallas_call(
        pack_kernel,
        grid_spec=pltpu.PrefetchScalarGridSpec(
            num_scalar_prefetch=1,
            grid=(share // step,),
            in_specs=[tile(0), tile(-1), tile(1)],
            out_specs=pl.BlockSpec((rows + 2, step, LANES), lambda block, place_ref: (0, block, 0)),
            scratch_shapes=[pltpu.VMEM((step * rows, LANES), jnp.float32)] * 2,
        ),
        out_shape=jax.ShapeDtypeStruct((rows + 2, share, LANES), jnp.bfloat16),
        name="pack",
    )(place, density, density, density)


def unpack_kernel(devices, part, parts, place, *refs):
    blocks, out_ref, wide, staged, sems = refs[:devices], *refs[-4:]
    rows, share, _ = blocks[0].shape
    copies = []
    for shift in range(devices):
        wide[...] = blocks[shift][...].astype(jnp.float32).reshape(rows * share, LANES)
        for orient in range(share):
            staged[shift, orient] = wide[pl.ds(orient, rows, stride=share), :].astype(jnp.bfloat16)
        tile = lax.rem(place[0] + shift, devices) * parts + part
        copies.append(
            pltpu.make_async_copy(
                staged.at[shift],
                out_ref.at[:, :, pl.ds(pl.multiple_of(tile * LANES, LANES), LANES)],
                sems.at[shift],
            )
        )
        copies[-1].start()
    for copy in copies:
        copy.wait()


def unpack(blocks, place, part, parts, shape, before):
    devices = len(blocks)
    rows, share, _ = blocks[0].shape
    earlier = () if before is None else (before,)
    return pl.pallas_call(
        functools.partial(unpack_kernel, devices, part, parts),
        in_specs=[pl.BlockSpec(memory_space=pltpu.SMEM)]
        + [pl.BlockSpec(memory_space=pltpu.VMEM)] * devices
        + [pl.BlockSpec(memory_space=pl.ANY)] * len(earlier),
        out_specs=pl.BlockSpec(memory_space=pl.ANY),
        scratch_shapes=[
            pltpu.VMEM((rows * share, LANES), jnp.float32),
            pltpu.VMEM((devices, share, rows, LANES), jnp.bfloat16),
            pltpu.SemaphoreType.DMA((devices,)),
        ],
        out_shape=jax.ShapeDtypeStruct(shape, jnp.bfloat16),
        input_output_aliases={1 + devices: 0} if earlier else {},
        compiler_params=pltpu.CompilerParams(vmem_limit_bytes=16 * 2**20),
        name="unpack",
    )(place, *blocks, *earlier)


def steps_kernel(devices, *refs):
    blocks = refs[:devices]
    above, below, kernel, turn, coefficients = refs[devices : devices + 5]
    outs = refs[devices + 5 : 2 * devices + 5]
    buffers = refs[2 * devices + 5 : 2 * devices + 7]
    waiting = refs[2 * devices + 7 :]
    share = blocks[0].shape[1]
    number = share * devices
    rows = outs[0].shape[0]
    tiles = number // LANES

    def transposed(value_of):
        return jnp.concatenate([value_of(part).astype(jnp.float32) for part in range(devices)], 0).T

    def piece(ref, index, part):
        return ref[index, part * share : (part + 1) * share]

    def fill(first, last, value_of):
        for row in range(first, last):
            cells = transposed(lambda part: value_of(row, part))
            for tile in range(tiles):
                buffers[0][row + REACH, tile, 2 * GROUP : 2 * GROUP + LANES] = cells[
                    :, tile * LANES : (tile + 1) * LANES
                ]

    def fill_sides(first, last, value_of):
        cells = transposed(value_of)
        for row in range(first, last):
            slot = row % GROUP
            left, right = (SLOT * slot - GROUP) % LANES, SLOT * slot
            for tile in range(tiles):
                lanes = slice(tile * LANES, (tile + 1) * LANES)
                buffers[0][row + REACH, tile, GROUP : 2 * GROUP] = cells[left : left + GROUP, lanes]
                buffers[0][row + REACH, tile, 2 * GROUP + LANES : 3 * GROUP + LANES] = cells[
                    right : right + GROUP, lanes
                ]

    fill(-REACH, 0, lambda row, part: piece(above, row + REACH, part))
    fill(0, rows, lambda row, part: blocks[part][1 + row])
    fill(rows, rows + REACH, lambda row, part: piece(below, 1 + row - rows, part))
    fill_sides(-REACH, 0, lambda part: piece(above, REACH, part))
    fill_sides(0, GROUP, lambda part: blocks[part][0])
    fill_sides(GROUP, rows, lambda part: blocks[part][rows + 1])
    fill_sides(rows, rows + REACH, lambda part: piece(below, 0, part))

    def advect(source, index, start, length, target):
        for tile in range(tiles):
            lanes = slice(tile * LANES, (tile + 1) * LANES)
            keep, by_row, by_column, row_sign, column_sign = (coefficients[k : k + 1, lanes] for k in range(5))
            forward_row = jnp.broadcast_to(row_sign, (length, LANES)) > 0
            forward_column = jnp.broadcast_to(column_sign, (length, LANES)) > 0
            for half in range(2):

                def at(row, column):
                    return source[index + half + row, tile, start + column : start + column + length]

                row_one = jnp.where(forward_row, at(-1, 0), at(1, 0))
                row_two = jnp.where(forward_row, at(-2, 0), at(2, 0))
                column_one = jnp.where(forward_column, at(0, -1), at(0, 1))
                column_two = jnp.where(forward_column, at(0, -2), at(0, 2))
                value = (
                    keep * at(0, 0)
                    + by_row * (row_one - 0.25 * row_two)
                    + by_column * (column_one - 0.25 * column_two)
                )
                target[half * length : (half + 1) * length, lanes] = value.astype(jnp.bfloat16)

    def rotate(values):
        potential = jnp.dot(values, kernel[...], preferred_element_type=jnp.float32)
        drifted = (values.astype(jnp.float32) * (1.0 + potential)).astype(jnp.bfloat16)
        turned = jnp.dot(drifted, turn[...], preferred_element_type=jnp.float32)
        return (values.astype(jnp.float32) + rotation_rate * turned).astype(jnp.bfloat16)

    for step in range(TIME_STEPS):
        source, target = buffers[step % 2], buffers[(step + 1) % 2]
        last = step == TIME_STEPS - 1
        start, length = (2 * GROUP, LANES) if last else (GROUP, LANES + 2 * GROUP)
        low, pairs = 2 * (step + 1), rows // 2 + REACH - 2 * (step + 1)

        def finish(slot, index):
            result = rotate(waiting[slot][: 2 * length]).astype(jnp.float32)
            for half in range(2):
                cells = result[half * length : (half + 1) * length]
                if last:
                    back = cells.T.astype(jnp.bfloat16)
                    for part in range(devices):
                        outs[part][index - REACH + half] = back[part * share : (part + 1) * share]
                else:
                    for tile in range(tiles):
                        target[index + half, tile, start : start + length] = cells[
                            :, tile * LANES : (tile + 1) * LANES
                        ]

        advect(source, low, start, length, waiting[0])

        @pl.loop(0, pairs // 2)
        def _(turn_index):
            index = low + 4 * turn_index
            advect(source, index + 2, start, length, waiting[1])
            finish(0, index)
            advect(source, jnp.minimum(index + 4, low + 2 * pairs - 2), start, length, waiting[0])
            finish(1, index + 2)


def three_steps(blocks, above, below, kernel, turn, coefficients):
    devices = len(blocks)
    rows, share, _ = blocks[0].shape
    rows -= 2
    number = share * devices
    cells = (rows + 2 * REACH) * LANES
    vmem = pl.BlockSpec(memory_space=pltpu.VMEM)
    operands = (*blocks, above, below, kernel, turn, coefficients)
    return pl.pallas_call(
        functools.partial(steps_kernel, devices),
        in_specs=[vmem] * len(operands),
        out_specs=[vmem] * devices,
        out_shape=[jax.ShapeDtypeStruct((rows, share, LANES), jnp.bfloat16)] * devices,
        scratch_shapes=[
            *[pltpu.VMEM((rows + 2 * REACH, number // LANES, LANES + 4 * GROUP, LANES), jnp.float32)] * 2,
            *[pltpu.VMEM((2 * (LANES + 2 * GROUP), number), jnp.bfloat16)] * 2,
        ],
        compiler_params=pltpu.CompilerParams(vmem_limit_bytes=48 * 2**20),
        cost_estimate=pl.CostEstimate(
            flops=12 * number * number * cells, bytes_accessed=8 * 2**20, transcendentals=0
        ),
        name="three_steps",
    )(*operands)


def blocked(density, kernel, neighbours, weights, signs, speeds):
    devices = lax.axis_size("ao")
    share, rows, columns = density.shape
    parts = columns // devices // LANES
    here = lax.axis_index("ao")
    place = here.astype(jnp.int32).reshape(1)

    packed = [[pack(density, place, shift, part, devices, parts) for shift in range(devices)] for part in range(parts)]

    def turned(value, dim):
        pieces = [
            lax.dynamic_slice_in_dim(value, lax.rem(here - shift + devices, devices) * share, share, dim)
            for shift in range(devices)
        ]
        return jnp.concatenate(pieces, dim)

    turn = turned(turned(stencil_matrix(neighbours, weights), 0), 1)
    kernel = turned(turned(kernel, 0), 1)
    signs, speeds = turned(signs, 1), turned(speeds, 1)

    coefficients = jnp.stack(
        [
            1.0 - 1.5 * (speeds[0] + speeds[1]),
            2.0 * speeds[0],
            2.0 * speeds[1],
            (signs[0] == 1).astype(jnp.float32),
            (signs[1] == 1).astype(jnp.float32),
        ]
    )
    kernel, turn = kernel.T, turn.T

    size = lax.axis_size("gx")
    up = [(i, (i + 1) % size) for i in range(size)]
    down = [(j, i) for i, j in up]
    def ahead(value, shift):
        return lax.ppermute(value, "ao", [(i, (i + shift) % devices) for i in range(devices)])

    def after(value, *earlier):
        return lax.optimization_barrier((value, *earlier))[0]

    received = []
    for part in range(parts):
        blocks = packed[part]
        if received:
            earlier = received[-1]
            blocks = [after(block, early) for block, early in zip(blocks, earlier)]
        received.append([blocks[0]] + [ahead(blocks[shift], shift) for shift in range(1, devices)])
    results = []
    for part in range(parts):
        arrived = received[part]
        edges = [after(block, results[-1]) for block in arrived] if results else arrived
        above = lax.ppermute(jnp.concatenate([block[-(REACH + 1) :] for block in edges], 1), "gx", up)
        below = lax.ppermute(jnp.concatenate([block[: REACH + 1] for block in edges], 1), "gx", down)
        results.append(three_steps(arrived, above, below, kernel, turn, coefficients))
    evolved = None
    for part in range(parts):
        result = results[part]
        returned = [result[0]] + [ahead(result[shift], devices - shift) for shift in range(1, devices)]
        evolved = unpack(returned, place, part, parts, density.shape, evolved)
    return evolved


def solution(mesh):
    in_specs = (P("ao", "gx", None), P(), P(), P(), P(), P())
    out_specs = P("ao", "gx", None)

    def run(density, *rest):
        share, rows, columns = (
            density.shape[0] // mesh.shape["ao"],
            density.shape[1] // mesh.shape["gx"],
            density.shape[2] // mesh.shape["ao"],
        )
        fits = columns % LANES == 0 and share % 32 == 0 and rows == 2 * GROUP
        body = jax.shard_map(
            blocked if fits else per_device, mesh=mesh, in_specs=in_specs, out_specs=out_specs, check_vma=False
        )
        return body(density, *rest)

    return run
```

profile of v0, /device:TPU:0, one launch (start us, length us, event | category | flops | bytes accessed | tf_op | source)
XLA Modules:
  0.0 165.9 jit_solution(6485985777155847595)
XLA Ops:
  0.0 2.7 %pack.15 = bf16[18,96,128]{2,1,0:T(8,128)(2,1)} custom-call(s32[1]{0:T(128)} %bitcast.place, bf16[96,16,1024]{2,1,0:T(8,128)(2,1)} %after_ref.15, bf16[96,16,1024]{2,1,0:T(8,128)(2,1)} %after_ref.15, bf16[96,16,1024]{2,1,0:T(8,128)(2,1)} %after_ref.15), custom_call_target="tpu_custom_call" | custom-call | tf_op jit(solution)/shard_map/pack/pallas_call | solution.py:138
  2.7 5.0 %collective-permute-start.4 = (bf16[18,96,128]{2,1,0:T(8,128)(2,1)}, bf16[18,96,128]{2,1,0:T(8,128)(2,1)S(1)}, u32[]{:S(2)}, u32[]{:S(2)}) collective-permute-start(bf16[18,96,128]{2,1,0:T(8,128)(2,1)} %pack.15), channel_id=1, source_target_pairs={{0,3},{1,0},{2,1},{3,2},{4,7},{5,4},{6,5},{7,6},{8,11},{9,8},{10,9... | collective-permute-start | bytes 1327112 | tf_op jit(solution)/shard_map/ppermute | solution.py:359
  7.7 2.7 %pack.11 = bf16[18,96,128]{2,1,0:T(8,128)(2,1)} custom-call(s32[1]{0:T(128)} %bitcast.place, bf16[96,16,1024]{2,1,0:T(8,128)(2,1)} %after_ref.15, bf16[96,16,1024]{2,1,0:T(8,128)(2,1)} %after_ref.15, bf16[96,16,1024]{2,1,0:T(8,128)(2,1)} %after_ref.15), custom_call_target="tpu_custom_call" | custom-call | tf_op jit(solution)/shard_map/pack/pallas_call | solution.py:138
  10.4 2.7 %pack.13 = bf16[18,96,128]{2,1,0:T(8,128)(2,1)} custom-call(s32[1]{0:T(128)} %bitcast.place, bf16[96,16,1024]{2,1,0:T(8,128)(2,1)} %after_ref.15, bf16[96,16,1024]{2,1,0:T(8,128)(2,1)} %after_ref.15, bf16[96,16,1024]{2,1,0:T(8,128)(2,1)} %after_ref.15), custom_call_target="tpu_custom_call" | custom-call | tf_op jit(solution)/shard_map/pack/pallas_call | solution.py:138
  14.1 2.7 %pack.9.refs_0_ = bf16[18,96,128]{2,1,0:T(8,128)(2,1)} custom-call(s32[1]{0:T(128)} %bitcast.place, bf16[96,16,1024]{2,1,0:T(8,128)(2,1)} %after_ref.15, bf16[96,16,1024]{2,1,0:T(8,128)(2,1)} %after_ref.15, bf16[96,16,1024]{2,1,0:T(8,128)(2,1)} %after_ref.15), custom_call_target="tpu_custom_call" | custom-call | tf_op jit(solution)/shard_map/pack/pallas_call | solution.py:138
  16.8 2.7 %pack.12 = bf16[18,96,128]{2,1,0:T(8,128)(2,1)} custom-call(s32[1]{0:T(128)} %bitcast.place, bf16[96,16,1024]{2,1,0:T(8,128)(2,1)} %after_ref.15, bf16[96,16,1024]{2,1,0:T(8,128)(2,1)} %after_ref.15, bf16[96,16,1024]{2,1,0:T(8,128)(2,1)} %after_ref.15), custom_call_target="tpu_custom_call" | custom-call | tf_op jit(solution)/shard_map/pack/pallas_call | solution.py:138
  19.5 2.7 %pack.10 = bf16[18,96,128]{2,1,0:T(8,128)(2,1)} custom-call(s32[1]{0:T(128)} %bitcast.place, bf16[96,16,1024]{2,1,0:T(8,128)(2,1)} %after_ref.15, bf16[96,16,1024]{2,1,0:T(8,128)(2,1)} %after_ref.15, bf16[96,16,1024]{2,1,0:T(8,128)(2,1)} %after_ref.15), custom_call_target="tpu_custom_call" | custom-call | tf_op jit(solution)/shard_map/pack/pallas_call | solution.py:138
  22.1 2.7 %pack.8.refs_0_ = bf16[18,96,128]{2,1,0:T(8,128)(2,1)} custom-call(s32[1]{0:T(128)} %bitcast.place, bf16[96,16,1024]{2,1,0:T(8,128)(2,1)} %after_ref.15, bf16[96,16,1024]{2,1,0:T(8,128)(2,1)} %after_ref.15, bf16[96,16,1024]{2,1,0:T(8,128)(2,1)} %after_ref.15), custom_call_target="tpu_custom_call" | custom-call | tf_op jit(solution)/shard_map/pack/pallas_call | solution.py:138
  24.8 2.7 %pack.14 = bf16[18,96,128]{2,1,0:T(8,128)(2,1)} custom-call(s32[1]{0:T(128)} %bitcast.place, bf16[96,16,1024]{2,1,0:T(8,128)(2,1)} %after_ref.15, bf16[96,16,1024]{2,1,0:T(8,128)(2,1)} %after_ref.15, bf16[96,16,1024]{2,1,0:T(8,128)(2,1)} %after_ref.15), custom_call_target="tpu_custom_call" | custom-call | tf_op jit(solution)/shard_map/pack/pallas_call | solution.py:138
  29.8 15.9 %collective-permute-done.2.refs_2_ = bf16[18,96,128]{2,1,0:T(8,128)(2,1)S(1)} collective-permute-done((bf16[18,96,128]{2,1,0:T(8,128)(2,1)}, bf16[18,96,128]{2,1,0:T(8,128)(2,1)S(1)}, u32[]{:S(2)}, u32[]{:S(2)}) %collective-permute-start.2) | collective-permute-done | bytes 442400 | tf_op jit(solution)/shard_map/ppermute | solution.py:359
  45.9 2.7 %collective-permute-start.7 = (bf16[7,384,128]{2,1,0:T(8,128)(2,1)S(1)}, bf16[7,384,128]{2,1,0:T(8,128)(2,1)S(1)}, u32[]{:S(2)}, u32[]{:S(2)}) collective-permute-start(bf16[7,384,128]{2,1,0:T(8,128)(2,1)S(1)} %pad_maximum_fusion.1), channel_id=1, source_target_pairs={{4,0},{8,4},{12,8},{16,12},{20,16},{24,20},{28,24},{0,28},{5,1},{9... | collective-permute-start | bytes 2064392 | tf_op jit(solution)/shard_map/ppermute | solution.py:376
  50.0 4.4 %collective-permute-start.5 = (bf16[18,96,128]{2,1,0:T(8,128)(2,1)S(1)}, bf16[18,96,128]{2,1,0:T(8,128)(2,1)S(1)}, u32[]{:S(2)}, u32[]{:S(2)}) collective-permute-start(bf16[18,96,128]{2,1,0:T(8,128)(2,1)S(1)} %copy-done.4), channel_id=1, source_target_pairs={{0,3},{1,0},{2,1},{3,2},{4,7},{5,4},{6,5},{7,6},{8,11},{9,8},{10,9... | collective-permute-start | bytes 1327112 | tf_op jit(solution)/shard_map/ppermute | solution.py:359
  55.2 7.2 %collective-permute-done.6.refs_4_ = bf16[7,384,128]{2,1,0:T(8,128)(2,1)S(1)} collective-permute-done((bf16[7,384,128]{2,1,0:T(8,128)(2,1)S(1)}, bf16[7,384,128]{2,1,0:T(8,128)(2,1)S(1)}, u32[]{:S(2)}, u32[]{:S(2)}) %collective-permute-start.6) | collective-permute-done | bytes 688160 | tf_op jit(solution)/shard_map/ppermute | solution.py:375
  62.6 17.9 %three_steps.2 = (bf16[16,96,128]{2,1,0:T(8,128)(2,1)S(1)}, bf16[16,96,128]{2,1,0:T(8,128)(2,1)S(1)}, bf16[16,96,128]{2,1,0:T(8,128)(2,1)S(1)}, bf16[16,96,128]{2,1,0:T(8,128)(2,1)S(1)}) custom-call(bf16[18,96,128]{2,1,0:T(8,128)(2,1)S(1)} %copy-done.1, bf16[18,96,128]{2,1,0:T(8,128)(2,1)S(1)} %collective-permute-done.refs_1_, ...), custom_call_target="tpu_custom_call" | custom-call | flops 6341787648 | bytes 8388608 | tf_op jit(solution)/shard_map/three_steps/pallas_call | solution.py:307
  80.5 10.1 %collective-permute-done.3.refs_2_ = bf16[18,96,128]{2,1,0:T(8,128)(2,1)S(1)} collective-permute-done((bf16[18,96,128]{2,1,0:T(8,128)(2,1)S(1)}, bf16[18,96,128]{2,1,0:T(8,128)(2,1)S(1)}, u32[]{:S(2)}, u32[]{:S(2)}) %collective-permute-start.3) | collective-permute-done | bytes 442400 | tf_op jit(solution)/shard_map/ppermute | solution.py:359
  90.9 2.7 %collective-permute-start.9 = (bf16[7,384,128]{2,1,0:T(8,128)(2,1)S(1)}, bf16[7,384,128]{2,1,0:T(8,128)(2,1)S(1)}, u32[]{:S(2)}, u32[]{:S(2)}) collective-permute-start(bf16[7,384,128]{2,1,0:T(8,128)(2,1)S(1)} %pad_maximum_fusion.3), channel_id=1, source_target_pairs={{4,0},{8,4},{12,8},{16,12},{20,16},{24,20},{28,24},{0,28},{5,1},{9... | collective-permute-start | bytes 2064392 | tf_op jit(solution)/shard_map/ppermute | solution.py:376
  93.6 2.6 %collective-permute-start.13 = (bf16[16,96,128]{2,1,0:T(8,128)(2,1)S(1)}, bf16[16,96,128]{2,1,0:T(8,128)(2,1)S(1)}, u32[]{:S(2)}, u32[]{:S(2)}) collective-permute-start(bf16[16,96,128]{2,1,0:T(8,128)(2,1)S(1)} %get-tuple-element.26), channel_id=1, source_target_pairs={{0,3},{1,0},{2,1},{3,2},{4,7},{5,4},{6,5},{7,6},{8,11},{9,8},{10,9... | collective-permute-start | bytes 1179656 | tf_op jit(solution)/shard_map/ppermute | solution.py:359
  96.8 11.7 %collective-permute-done.8.refs_4_ = bf16[7,384,128]{2,1,0:T(8,128)(2,1)S(1)} collective-permute-done((bf16[7,384,128]{2,1,0:T(8,128)(2,1)S(1)}, bf16[7,384,128]{2,1,0:T(8,128)(2,1)S(1)}, u32[]{:S(2)}, u32[]{:S(2)}) %collective-permute-start.8) | collective-permute-done | bytes 688160 | tf_op jit(solution)/shard_map/ppermute | solution.py:375
  108.6 17.9 %three_steps.3 = (bf16[16,96,128]{2,1,0:T(8,128)(2,1)S(1)}, bf16[16,96,128]{2,1,0:T(8,128)(2,1)S(1)}, bf16[16,96,128]{2,1,0:T(8,128)(2,1)S(1)}, bf16[16,96,128]{2,1,0:T(8,128)(2,1)S(1)}) custom-call(bf16[18,96,128]{2,1,0:T(8,128)(2,1)S(1)} %copy-done, bf16[18,96,128]{2,1,0:T(8,128)(2,1)S(1)} %collective-permute-done.1.refs_1_, ...), custom_call_target="tpu_custom_call" | custom-call | flops 6341787648 | bytes 8388608 | tf_op jit(solution)/shard_map/three_steps/pallas_call | solution.py:307
  126.5 2.7 %collective-permute-start.10 = (bf16[16,96,128]{2,1,0:T(8,128)(2,1)S(1)}, bf16[16,96,128]{2,1,0:T(8,128)(2,1)S(1)}, u32[]{:S(2)}, u32[]{:S(2)}) collective-permute-start(bf16[16,96,128]{2,1,0:T(8,128)(2,1)S(1)} %get-tuple-element.34), channel_id=1, source_target_pairs={{0,3},{1,0},{2,1},{3,2},{4,7},{5,4},{6,5},{7,6},{8,11},{9,8},{10,9... | collective-permute-start | bytes 1179656 | tf_op jit(solution)/shard_map/ppermute | solution.py:359
  129.9 2.7 %unpack.2.refs_4_ = bf16[96,16,1024]{2,1,0:T(8,128)(2,1)} custom-call(s32[1]{0:T(128)} %bitcast.place, bf16[16,96,128]{2,1,0:T(8,128)(2,1)S(1)} %get-tuple-element.25.refs_0_, bf16[16,96,128]{2,1,0:T(8,128)(2,1)S(1)} %collective-permute-done.13.refs_1_, bf16[16,96,128]{2,1,0:T(8,128)(2,1)S(1)} %collective-permute-done.14.refs_2_, ...), custom_call_target="tpu_custom_call" | custom-call | tf_op jit(solution)/shard_map/unpack/pallas_call | solution.py:177
  132.5 7.2 %collective-permute-done.10.refs_1_ = bf16[16,96,128]{2,1,0:T(8,128)(2,1)S(1)} collective-permute-done((bf16[16,96,128]{2,1,0:T(8,128)(2,1)S(1)}, bf16[16,96,128]{2,1,0:T(8,128)(2,1)S(1)}, u32[]{:S(2)}, u32[]{:S(2)}) %collective-permute-start.10) | collective-permute-done | bytes 393248 | tf_op jit(solution)/shard_map/ppermute | solution.py:359
  139.7 23.3 %collective-permute-done.11.refs_2_ = bf16[16,96,128]{2,1,0:T(8,128)(2,1)S(1)} collective-permute-done((bf16[16,96,128]{2,1,0:T(8,128)(2,1)S(1)}, bf16[16,96,128]{2,1,0:T(8,128)(2,1)S(1)}, u32[]{:S(2)}, u32[]{:S(2)}) %collective-permute-start.11) | collective-permute-done | bytes 393248 | tf_op jit(solution)/shard_map/ppermute | solution.py:359
  163.0 2.7 %unpack.3 = bf16[96,16,1024]{2,1,0:T(8,128)(2,1)} custom-call(s32[1]{0:T(128)} %bitcast.place, bf16[16,96,128]{2,1,0:T(8,128)(2,1)S(1)} %get-tuple-element.33.refs_0_, bf16[16,96,128]{2,1,0:T(8,128)(2,1)S(1)} %collective-permute-done.10.refs_1_, bf16[16,96,128]{2,1,0:T(8,128)(2,1)S(1)} %collective-permute-done.11.refs_2_, ...), custom_call_target="tpu_custom_call", output_to_operand_aliasing={{}: (5, {})} | custom-call | tf_op jit(solution)/shard_map/unpack/pallas_call | solution.py:177
  (75 shorter events, 7.2 us)
Async XLA Ops:
  2.7 27.1 %collective-permute-start.4 = (bf16[18,96,128]{2,1,0:T(8,128)(2,1)}, bf16[18,96,128]{2,1,0:T(8,128)(2,1)S(1)}, u32[]{:S(2)}, u32[]{:S(2)}) collective-permute-start(bf16[18,96,128]{2,1,0:T(8,128)(2,1)} %pack.15), channel_id=1, source_target_pairs={{0,3},{1,0},{2,1},{3,2},{4,7},{5,4},{6,5},{7,6},{8,11},{9,8},{10,9... | collective-permute-start | bytes 1327112 | tf_op jit(solution)/shard_map/ppermute | solution.py:359
  10.4 3.7 %copy-start.6 = (s32[384,6]{0,1:T(8,128)S(1)}, s32[384,6]{0,1:T(8,128)}, u32[]{:S(2)}) copy-start(s32[384,6]{0,1:T(8,128)} %param.9) | copy-start | bytes 27652
  10.4 19.4 %collective-permute-start = (bf16[18,96,128]{2,1,0:T(8,128)(2,1)}, bf16[18,96,128]{2,1,0:T(8,128)(2,1)S(1)}, u32[]{:S(2)}, u32[]{:S(2)}) collective-permute-start(bf16[18,96,128]{2,1,0:T(8,128)(2,1)} %pack.11), channel_id=1, source_target_pairs={{0,1},{1,2},{2,3},{3,0},{4,5},{5,6},{6,7},{7,4},{8,9},{9,10},{10,1... | collective-permute-start | bytes 1327112 | tf_op jit(solution)/shard_map/ppermute | solution.py:359
  13.1 32.6 %collective-permute-start.2 = (bf16[18,96,128]{2,1,0:T(8,128)(2,1)}, bf16[18,96,128]{2,1,0:T(8,128)(2,1)S(1)}, u32[]{:S(2)}, u32[]{:S(2)}) collective-permute-start(bf16[18,96,128]{2,1,0:T(8,128)(2,1)} %pack.13), channel_id=1, source_target_pairs={{0,2},{1,3},{2,0},{3,1},{4,6},{5,7},{6,4},{7,5},{8,10},{9,11},{10,... | collective-permute-start | bytes 1327112 | tf_op jit(solution)/shard_map/ppermute | solution.py:359
  24.8 2.8 %copy-start.8 = (s32[2,384]{1,0:T(2,128)S(1)}, s32[2,384]{1,0:T(2,128)}, u32[]{:S(2)}) copy-start(s32[2,384]{1,0:T(2,128)} %param.10) | copy-start | bytes 9220
  24.8 2.9 %copy-start.9 = (f32[2,384]{1,0:T(2,128)S(1)}, f32[2,384]{1,0:T(2,128)}, u32[]{:S(2)}) copy-start(f32[2,384]{1,0:T(2,128)} %param.11) | copy-start | bytes 9220
  24.8 3.1 %copy-start.5 = (bf16[384,384]{1,0:T(8,128)(2,1)S(1)}, bf16[384,384]{1,0:T(8,128)(2,1)}, u32[]{:S(2)}) copy-start(bf16[384,384]{1,0:T(8,128)(2,1)} %param.7) | copy-start | bytes 884740
  24.8 3.7 %copy-start.7 = (s32[384,6]{0,1:T(8,128)S(1)}, s32[384,6]{0,1:T(8,128)}, u32[]{:S(2)}) copy-start(s32[384,6]{0,1:T(8,128)} %param.8) | copy-start | bytes 27652
  45.8 16.7 %collective-permute-start.6 = (bf16[7,384,128]{2,1,0:T(8,128)(2,1)S(1)}, bf16[7,384,128]{2,1,0:T(8,128)(2,1)S(1)}, u32[]{:S(2)}, u32[]{:S(2)}) collective-permute-start(bf16[7,384,128]{2,1,0:T(8,128)(2,1)S(1)} %pad_maximum_fusion), channel_id=1, source_target_pairs={{0,4},{4,8},{8,12},{12,16},{16,20},{20,24},{24,28},{28,0},{1,5},{5... | collective-permute-start | bytes 2064392 | tf_op jit(solution)/shard_map/ppermute | solution.py:375
  45.9 16.7 %collective-permute-start.7 = (bf16[7,384,128]{2,1,0:T(8,128)(2,1)S(1)}, bf16[7,384,128]{2,1,0:T(8,128)(2,1)S(1)}, u32[]{:S(2)}, u32[]{:S(2)}) collective-permute-start(bf16[7,384,128]{2,1,0:T(8,128)(2,1)S(1)} %pad_maximum_fusion.1), channel_id=1, source_target_pairs={{4,0},{8,4},{12,8},{16,12},{20,16},{24,20},{28,24},{0,28},{5,1},{9... | collective-permute-start | bytes 2064392 | tf_op jit(solution)/shard_map/ppermute | solution.py:376
  49.0 5.4 %copy-start.2 = (bf16[18,96,128]{2,1,0:T(8,128)(2,1)S(1)}, bf16[18,96,128]{2,1,0:T(8,128)(2,1)}, u32[]{:S(2)}) copy-start(bf16[18,96,128]{2,1,0:T(8,128)(2,1)} %pack.10) | copy-start | bytes 1327108
  49.0 5.4 %copy-start.3 = (bf16[18,96,128]{2,1,0:T(8,128)(2,1)S(1)}, bf16[18,96,128]{2,1,0:T(8,128)(2,1)}, u32[]{:S(2)}) copy-start(bf16[18,96,128]{2,1,0:T(8,128)(2,1)} %pack.12) | copy-start | bytes 1327108
  50.0 40.6 %copy-start = (bf16[18,96,128]{2,1,0:T(8,128)(2,1)S(1)}, bf16[18,96,128]{2,1,0:T(8,128)(2,1)}, u32[]{:S(2)}) copy-start(bf16[18,96,128]{2,1,0:T(8,128)(2,1)} %pack.8.refs_0_) | copy-start | bytes 1327108
  50.0 30.5 %collective-permute-start.5 = (bf16[18,96,128]{2,1,0:T(8,128)(2,1)S(1)}, bf16[18,96,128]{2,1,0:T(8,128)(2,1)S(1)}, u32[]{:S(2)}, u32[]{:S(2)}) collective-permute-start(bf16[18,96,128]{2,1,0:T(8,128)(2,1)S(1)} %copy-done.4), channel_id=1, source_target_pairs={{0,3},{1,0},{2,1},{3,2},{4,7},{5,4},{6,5},{7,6},{8,11},{9,8},{10,9... | collective-permute-start | bytes 1327112 | tf_op jit(solution)/shard_map/ppermute | solution.py:359
  54.4 36.2 %collective-permute-start.1 = (bf16[18,96,128]{2,1,0:T(8,128)(2,1)S(1)}, bf16[18,96,128]{2,1,0:T(8,128)(2,1)S(1)}, u32[]{:S(2)}, u32[]{:S(2)}) collective-permute-start(bf16[18,96,128]{2,1,0:T(8,128)(2,1)S(1)} %copy-done.2), channel_id=1, source_target_pairs={{0,1},{1,2},{2,3},{3,0},{4,5},{5,6},{6,7},{7,4},{8,9},{9,10},{10,1... | collective-permute-start | bytes 1327112 | tf_op jit(solution)/shard_map/ppermute | solution.py:359
  54.4 36.2 %collective-permute-start.3 = (bf16[18,96,128]{2,1,0:T(8,128)(2,1)S(1)}, bf16[18,96,128]{2,1,0:T(8,128)(2,1)S(1)}, u32[]{:S(2)}, u32[]{:S(2)}) collective-permute-start(bf16[18,96,128]{2,1,0:T(8,128)(2,1)S(1)} %copy-done.3), channel_id=1, source_target_pairs={{0,2},{1,3},{2,0},{3,1},{4,6},{5,7},{6,4},{7,5},{8,10},{9,11},{10,... | collective-permute-start | bytes 1327112 | tf_op jit(solution)/shard_map/ppermute | solution.py:359
  90.8 17.8 %collective-permute-start.8 = (bf16[7,384,128]{2,1,0:T(8,128)(2,1)S(1)}, bf16[7,384,128]{2,1,0:T(8,128)(2,1)S(1)}, u32[]{:S(2)}, u32[]{:S(2)}) collective-permute-start(bf16[7,384,128]{2,1,0:T(8,128)(2,1)S(1)} %pad_maximum_fusion.2), channel_id=1, source_target_pairs={{0,4},{4,8},{8,12},{12,16},{16,20},{20,24},{24,28},{28,0},{1,5},{5... | collective-permute-start | bytes 2064392 | tf_op jit(solution)/shard_map/ppermute | solution.py:375
  90.9 17.6 %collective-permute-start.9 = (bf16[7,384,128]{2,1,0:T(8,128)(2,1)S(1)}, bf16[7,384,128]{2,1,0:T(8,128)(2,1)S(1)}, u32[]{:S(2)}, u32[]{:S(2)}) collective-permute-start(bf16[7,384,128]{2,1,0:T(8,128)(2,1)S(1)} %pad_maximum_fusion.3), channel_id=1, source_target_pairs={{4,0},{8,4},{12,8},{16,12},{20,16},{24,20},{28,24},{0,28},{5,1},{9... | collective-permute-start | bytes 2064392 | tf_op jit(solution)/shard_map/ppermute | solution.py:376
  93.6 35.6 %collective-permute-start.13 = (bf16[16,96,128]{2,1,0:T(8,128)(2,1)S(1)}, bf16[16,96,128]{2,1,0:T(8,128)(2,1)S(1)}, u32[]{:S(2)}, u32[]{:S(2)}) collective-permute-start(bf16[16,96,128]{2,1,0:T(8,128)(2,1)S(1)} %get-tuple-element.26), channel_id=1, source_target_pairs={{0,3},{1,0},{2,1},{3,2},{4,7},{5,4},{6,5},{7,6},{8,11},{9,8},{10,9... | collective-permute-start | bytes 1179656 | tf_op jit(solution)/shard_map/ppermute | solution.py:359
  96.3 33.6 %collective-permute-start.14 = (bf16[16,96,128]{2,1,0:T(8,128)(2,1)S(1)}, bf16[16,96,128]{2,1,0:T(8,128)(2,1)S(1)}, u32[]{:S(2)}, u32[]{:S(2)}) collective-permute-start(bf16[16,96,128]{2,1,0:T(8,128)(2,1)S(1)} %get-tuple-element.27), channel_id=1, source_target_pairs={{0,2},{1,3},{2,0},{3,1},{4,6},{5,7},{6,4},{7,5},{8,10},{9,11},{10,... | collective-permute-start | bytes 1179656 | tf_op jit(solution)/shard_map/ppermute | solution.py:359
  96.3 33.6 %collective-permute-start.15 = (bf16[16,96,128]{2,1,0:T(8,128)(2,1)S(1)}, bf16[16,96,128]{2,1,0:T(8,128)(2,1)S(1)}, u32[]{:S(2)}, u32[]{:S(2)}) collective-permute-start(bf16[16,96,128]{2,1,0:T(8,128)(2,1)S(1)} %get-tuple-element.28), channel_id=1, source_target_pairs={{0,1},{1,2},{2,3},{3,0},{4,5},{5,6},{6,7},{7,4},{8,9},{9,10},{10,1... | collective-permute-start | bytes 1179656 | tf_op jit(solution)/shard_map/ppermute | solution.py:359
  126.5 13.2 %collective-permute-start.10 = (bf16[16,96,128]{2,1,0:T(8,128)(2,1)S(1)}, bf16[16,96,128]{2,1,0:T(8,128)(2,1)S(1)}, u32[]{:S(2)}, u32[]{:S(2)}) collective-permute-start(bf16[16,96,128]{2,1,0:T(8,128)(2,1)S(1)} %get-tuple-element.34), channel_id=1, source_target_pairs={{0,3},{1,0},{2,1},{3,2},{4,7},{5,4},{6,5},{7,6},{8,11},{9,8},{10,9... | collective-permute-start | bytes 1179656 | tf_op jit(solution)/shard_map/ppermute | solution.py:359
  129.2 33.8 %collective-permute-start.11 = (bf16[16,96,128]{2,1,0:T(8,128)(2,1)S(1)}, bf16[16,96,128]{2,1,0:T(8,128)(2,1)S(1)}, u32[]{:S(2)}, u32[]{:S(2)}) collective-permute-start(bf16[16,96,128]{2,1,0:T(8,128)(2,1)S(1)} %get-tuple-element.35), channel_id=1, source_target_pairs={{0,2},{1,3},{2,0},{3,1},{4,6},{5,7},{6,4},{7,5},{8,10},{9,11},{10,... | collective-permute-start | bytes 1179656 | tf_op jit(solution)/shard_map/ppermute | solution.py:359
  129.2 33.8 %collective-permute-start.12 = (bf16[16,96,128]{2,1,0:T(8,128)(2,1)S(1)}, bf16[16,96,128]{2,1,0:T(8,128)(2,1)S(1)}, u32[]{:S(2)}, u32[]{:S(2)}) collective-permute-start(bf16[16,96,128]{2,1,0:T(8,128)(2,1)S(1)} %get-tuple-element.36), channel_id=1, source_target_pairs={{0,1},{1,2},{2,3},{3,0},{4,5},{5,6},{6,7},{7,4},{8,9},{9,10},{10,1... | collective-permute-start | bytes 1179656 | tf_op jit(solution)/shard_map/ppermute | solution.py:359
  (2 other events, 2.2 us)
where the time goes:
time: 166 us
  waiting for transfers between devices  75.6 us (46%)
  Pallas kernels  62.6 us (38%)
  starting transfers between devices  23.2 us (14%)
  local copies, waits for them, and re-layouts  2.15 us (1%)
  other arithmetic  1.74 us (1%)
    ppermute x12, waiting for transfers between devices, ahead(): lax.ppermute(value, 'ao', [(i, (i + shift) % devices) for i in range(devi...  56.5 us
    pallas_call x2, Pallas kernels, three_steps(): pl.pallas_call(functools.partial(steps_kernel, devices), in_specs=[vmem]...  35.8 us
    pallas_call x8, Pallas kernels, pack(): pl.pallas_call(pack_kernel, grid_spec=pltpu.PrefetchScalarGridSpec(num_sc...  21.5 us
    ppermute x2, waiting for transfers between devices, blocked(): lax.ppermute(jnp.concatenate([block[-(REACH + 1):] for block in edges], 1...  19 us
    ppermute x12, starting transfers between devices, ahead(): lax.ppermute(value, 'ao', [(i, (i + shift) % devices) for i in range(devi...  17.8 us
    ppermute x2, starting transfers between devices, blocked(): lax.ppermute(jnp.concatenate([block[:REACH + 1] for block in edges], 1),...  5.35 us
    pallas_call x2, Pallas kernels, unpack(): pl.pallas_call(functools.partial(unpack_kernel, devices, part, parts), in...  5.35 us
  transfers between devices with their start and end apart: 16, of which 7 were waited for; matrix products, arithmetic and copies ran while one was open for 2% of the time, Pallas kernels for 35%

commit v1 on v0

--- a/solution.py
+++ b/solution.py
@@ -102,23 +102,30 @@
 SLOT = LANES // GROUP
 
 
-def pack_kernel(place, main_ref, before_ref, after_ref, out_ref, main, sides):
+def pack_kernel(place, main_ref, *refs):
+    *side_refs, out_ref, main, sides = refs
     orients, rows, _ = main_ref.shape
+    both = len(side_refs) == 2
+    width = SLOT if both else GROUP
+    slots = LANES // width
     lane = lax.broadcasted_iota(jnp.int32, (orients, LANES), 1)
-    main[...] = main_ref[...].astype(jnp.float32).reshape(orients * rows, LANES)
-    wide_lane = lax.broadcasted_iota(jnp.int32, (orients * rows, LANES), 1)
-    sides[...] = jnp.where(
-        wide_lane < LANES // 2,
-        after_ref[...].astype(jnp.float32).reshape(orients * rows, LANES),
-        before_ref[...].astype(jnp.float32).reshape(orients * rows, LANES),
-    )
-    owner = ((lane + SLOT // 2) % LANES) // SLOT
-    for group in range(rows // GROUP):
+    owner = ((lane + SLOT // 2) % LANES) // SLOT if both else lane // GROUP
+
+    def flat(ref):
+        return ref[...].astype(jnp.float32).reshape(orients * rows, LANES)
+
+    main[...] = flat(main_ref)
+    if both:
+        wide_lane = lax.broadcasted_iota(jnp.int32, (orients * rows, LANES), 1)
+        sides[...] = jnp.where(wide_lane < LANES // 2, flat(side_refs[0]), flat(side_refs[1]))
+    else:
+        sides[...] = flat(side_refs[0])
+    for group in range(rows // slots):
         packed = jnp.zeros((orients, LANES), jnp.float32)
-        for slot in range(GROUP):
-            row = group * GROUP + slot
+        for slot in range(slots):
+            row = group * slots + slot
             out_ref[1 + row] = main[pl.ds(row, orients, stride=rows), :].astype(jnp.bfloat16)
-            edge = pltpu.roll(sides[pl.ds(row, orients, stride=rows), :], SLOT * slot, 1)
+            edge = pltpu.roll(sides[pl.ds(row, orients, stride=rows), :], width * slot, 1)
             packed = jnp.where(owner == slot, edge, packed)
         out_ref[0 if group == 0 else rows + 1] = packed.astype(jnp.bfloat16)
 
@@ -126,27 +133,28 @@
 def pack(density, place, shift, part, devices, parts):
     share, rows, columns = density.shape
     tiles = columns // LANES
-    step = share
+    offsets = (0, 1) if part else (0, 1, -1)
+    length = rows + (1 if part else 2)
 
     def tile(offset):
         def index(block, place_ref):
             target = lax.rem(place_ref[0] + shift, devices)
             return block, 0, lax.rem(target * parts + part + offset + tiles, tiles)
 
-        return pl.BlockSpec((step, rows, LANES), index)
+        return pl.BlockSpec((share, rows, LANES), index)
 
     return pl.pallas_call(
         pack_kernel,
         grid_spec=pltpu.PrefetchScalarGridSpec(
             num_scalar_prefetch=1,
-            grid=(share // step,),
-            in_specs=[tile(0), tile(-1), tile(1)],
-            out_specs=pl.BlockSpec((rows + 2, step, LANES), lambda block, place_ref: (0, block, 0)),
-            scratch_shapes=[pltpu.VMEM((step * rows, LANES), jnp.float32)] * 2,
+            grid=(1,),
+            in_specs=[tile(offset) for offset in offsets],
+            out_specs=pl.BlockSpec((length, share, LANES), lambda block, place_ref: (0, block, 0)),
+            scratch_shapes=[pltpu.VMEM((share * rows, LANES), jnp.float32)] * 2,
         ),
-        out_shape=jax.ShapeDtypeStruct((rows + 2, share, LANES), jnp.bfloat16),
+        out_shape=jax.ShapeDtypeStruct((length, share, LANES), jnp.bfloat16),
         name="pack",
-    )(place, density, density, density)
+    )(place, *[density] * len(offsets))
 
 
 def unpack_kernel(devices, part, parts, place, *refs):
@@ -192,12 +200,13 @@
     )(place, *blocks, *earlier)
 
 
-def steps_kernel(devices, *refs):
-    blocks = refs[:devices]
-    above, below, kernel, turn, coefficients = refs[devices : devices + 5]
-    outs = refs[devices + 5 : 2 * devices + 5]
-    buffers = refs[2 * devices + 5 : 2 * devices + 7]
-    waiting = refs[2 * devices + 7 :]
+def steps_kernel(devices, joined, followed, *refs):
+    blocks, refs = refs[:devices], refs[devices:]
+    above, below, kernel, turn, coefficients = refs[:5]
+    edge_in, refs = (refs[5], refs[6:]) if joined else (None, refs[5:])
+    outs, refs = refs[:devices], refs[devices:]
+    edge_out, refs = (refs[0], refs[1:]) if followed else (None, refs)
+    buffers, waiting = refs[:2], refs[2:]
     share = blocks[0].shape[1]
     number = share * devices
     rows = outs[0].shape[0]
@@ -213,28 +222,38 @@
         for row in range(first, last):
             cells = transposed(lambda part: value_of(row, part))
             for tile in range(tiles):
-                buffers[0][row + REACH, tile, 2 * GROUP : 2 * GROUP + LANES] = cells[
-                    :, tile * LANES : (tile + 1) * LANES
-                ]
+                lanes = slice(tile * LANES, (tile + 1) * LANES)
+                buffers[0][row + REACH, tile, 2 * GROUP : 2 * GROUP + LANES] = cells[:, lanes]
+                if followed:
+                    edge_out[row + REACH, tile] = cells[LANES - GROUP :, lanes]
 
     def fill_sides(first, last, value_of):
         cells = transposed(value_of)
         for row in range(first, last):
-            slot = row % GROUP
-            left, right = (SLOT * slot - GROUP) % LANES, SLOT * slot
+            if joined:
+                right = GROUP * (row % rows)
+            else:
+                right = SLOT * (row % GROUP)
+                left = (right - GROUP) % LANES
             for tile in range(tiles):
                 lanes = slice(tile * LANES, (tile + 1) * LANES)
-                buffers[0][row + REACH, tile, GROUP : 2 * GROUP] = cells[left : left + GROUP, lanes]
+                buffers[0][row + REACH, tile, GROUP : 2 * GROUP] = (
+                    edge_in[row + REACH, tile] if joined else cells[left : left + GROUP, lanes]
+                )
                 buffers[0][row + REACH, tile, 2 * GROUP + LANES : 3 * GROUP + LANES] = cells[
                     right : right + GROUP, lanes
                 ]
 
-    fill(-REACH, 0, lambda row, part: piece(above, row + REACH, part))
+    lead = REACH + 1 if joined else REACH
+    fill(-REACH, 0, lambda row, part: piece(above, row + lead, part))
     fill(0, rows, lambda row, part: blocks[part][1 + row])
     fill(rows, rows + REACH, lambda row, part: piece(below, 1 + row - rows, part))
-    fill_sides(-REACH, 0, lambda part: piece(above, REACH, part))
-    fill_sides(0, GROUP, lambda part: blocks[part][0])
-    fill_sides(GROUP, rows, lambda part: blocks[part][rows + 1])
+    fill_sides(-REACH, 0, lambda part: piece(above, 0 if joined else REACH, part))
+    if joined:
+        fill_sides(0, rows, lambda part: blocks[part][0])
+    else:
+        fill_sides(0, GROUP, lambda part: blocks[part][0])
+        fill_sides(GROUP, rows, lambda part: blocks[part][rows + 1])
     fill_sides(rows, rows + REACH, lambda part: piece(below, 0, part))
 
     def advect(source, index, start, length, target):
@@ -296,29 +315,33 @@
             finish(1, index + 2)
 
 
-def three_steps(blocks, above, below, kernel, turn, coefficients):
+def three_steps(blocks, above, below, kernel, turn, coefficients, rows, edge, followed):
     devices = len(blocks)
-    rows, share, _ = blocks[0].shape
-    rows -= 2
+    share = blocks[0].shape[1]
     number = share * devices
-    cells = (rows + 2 * REACH) * LANES
+    tiles = number // LANES
+    tall = rows + 2 * REACH
     vmem = pl.BlockSpec(memory_space=pltpu.VMEM)
-    operands = (*blocks, above, below, kernel, turn, coefficients)
-    return pl.pallas_call(
-        functools.partial(steps_kernel, devices),
+    operands = (*blocks, above, below, kernel, turn, coefficients, *([] if edge is None else [edge]))
+    out_shape = [jax.ShapeDtypeStruct((rows, share, LANES), jnp.bfloat16)] * devices
+    if followed:
+        out_shape.append(jax.ShapeDtypeStruct((tall, tiles, GROUP, LANES), jnp.float32))
+    outs = pl.pallas_call(
+        functools.partial(steps_kernel, devices, edge is not None, followed),
         in_specs=[vmem] * len(operands),
-        out_specs=[vmem] * devices,
-        out_shape=[jax.ShapeDtypeStruct((rows, share, LANES), jnp.bfloat16)] * devices,
+        out_specs=[vmem] * len(out_shape),
+        out_shape=out_shape,
         scratch_shapes=[
-            *[pltpu.VMEM((rows + 2 * REACH, number // LANES, LANES + 4 * GROUP, LANES), jnp.float32)] * 2,
+            *[pltpu.VMEM((tall, tiles, LANES + 4 * GROUP, LANES), jnp.float32)] * 2,
             *[pltpu.VMEM((2 * (LANES + 2 * GROUP), number), jnp.bfloat16)] * 2,
         ],
         compiler_params=pltpu.CompilerParams(vmem_limit_bytes=48 * 2**20),
         cost_estimate=pl.CostEstimate(
-            flops=12 * number * number * cells, bytes_accessed=8 * 2**20, transcendentals=0
+            flops=12 * number * number * tall * LANES, bytes_accessed=8 * 2**20, transcendentals=0
         ),
         name="three_steps",
     )(*operands)
+    return outs[:devices], outs[devices] if followed else None
 
 
 def blocked(density, kernel, neighbours, weights, signs, speeds):
@@ -368,13 +391,25 @@
             earlier = received[-1]
             blocks = [after(block, early) for block, early in zip(blocks, earlier)]
         received.append([blocks[0]] + [ahead(blocks[shift], shift) for shift in range(1, devices)])
-    results = []
+    results, edge = [], None
     for part in range(parts):
         arrived = received[part]
-        edges = [after(block, results[-1]) for block in arrived] if results else arrived
-        above = lax.ppermute(jnp.concatenate([block[-(REACH + 1) :] for block in edges], 1), "gx", up)
-        below = lax.ppermute(jnp.concatenate([block[: REACH + 1] for block in edges], 1), "gx", down)
-        results.append(three_steps(arrived, above, below, kernel, turn, coefficients))
+        ends = [after(block, results[-1]) for block in arrived] if results else arrived
+
+        def joint(first, last):
+            return jnp.concatenate([block[first:last] for block in ends], 1)
+
+        length = ends[0].shape[0]
+        if part:
+            upper = jnp.concatenate([joint(0, 1), joint(length - REACH, length)], 0)
+        else:
+            upper = joint(length - REACH - 1, length)
+        above = lax.ppermute(upper, "gx", up)
+        below = lax.ppermute(joint(0, REACH + 1), "gx", down)
+        result, edge = three_steps(
+            arrived, above, below, kernel, turn, coefficients, rows, edge, part + 1 < parts
+        )
+        results.append(result)
     evolved = None
     for part in range(parts):
         result = results[part]

time: 166 us -> 163 us (0.982)
  starting transfers between devices: 23.2 us -> 20.7 us
  waiting for transfers between devices: 75.6 us -> 73.7 us
    ppermute x12, waiting for transfers between devices: 56.5 us -> 52.7 us  [ahead(): lax.ppermute(value, 'ao', [(i, (i + shift) % devices) for i in range(devi...]
    ppermute x4, starting transfers between devices: 5.47 us -> 2.85 us  [the longest x2 2.73 us: blocked(): below = lax.ppermute(joint(0, REACH + 1), 'gx', down)]
    ppermute x4, waiting for transfers between devices: 19.1 us -> 21 us  [the longest x2 11.1 us: blocked(): above = lax.ppermute(upper, 'gx', up)]
  transfers between devices with their start and end apart: 16 -> 16, of which waited for: 7 -> 8; matrix products, arithmetic and copies ran while one was open for 2% -> 2% of each run, Pallas kernels for 35% -> 36%
where the time goes in v1:
time: 163 us
  waiting for transfers between devices  73.7 us (45%)
  Pallas kernels  63.2 us (39%)
  starting transfers between devices  20.7 us (13%)
  local copies, waits for them, and re-layouts  2.83 us (2%)
  other arithmetic  1.74 us (1%)
    ppermute x12, waiting for transfers between devices, ahead(): lax.ppermute(value, 'ao', [(i, (i + shift) % devices) for i in range(devi...  52.7 us
    pallas_call x2, Pallas kernels, three_steps(): pl.pallas_call(functools.partial(steps_kernel, devices, edge is not None,...  37.2 us
    pallas_call x8, Pallas kernels, pack(): pl.pallas_call(pack_kernel, grid_spec=pltpu.PrefetchScalarGridSpec(num_sc...  20.7 us
    ppermute x12, starting transfers between devices, ahead(): lax.ppermute(value, 'ao', [(i, (i + shift) % devices) for i in range(devi...  17.8 us
    ppermute x2, waiting for transfers between devices, blocked(): above = lax.ppermute(upper, 'gx', up)  11.1 us
    ppermute x2, waiting for transfers between devices, blocked(): below = lax.ppermute(joint(0, REACH + 1), 'gx', down)  9.98 us
    pallas_call x2, Pallas kernels, unpack(): pl.pallas_call(functools.partial(unpack_kernel, devices, part, parts), in...  5.37 us
  transfers between devices with their start and end apart: 16, of which 8 were waited for; matrix products, arithmetic and copies ran while one was open for 2% of the time, Pallas kernels for 36%

profile of v1, /device:TPU:0, one launch (start us, length us, event | category | flops | bytes accessed | tf_op | source)
XLA Modules:
  0.0 162.7 jit_solution(14558754923496214897)
XLA Ops:
  0.0 2.6 %pack.15 = bf16[18,96,128]{2,1,0:T(8,128)(2,1)} custom-call(s32[1]{0:T(128)} %bitcast.place, bf16[96,16,1024]{2,1,0:T(8,128)(2,1)} %refs_1_.7, bf16[96,16,1024]{2,1,0:T(8,128)(2,1)} %refs_1_.7, bf16[96,16,1024]{2,1,0:T(8,128)(2,1)} %refs_1_.7), custom_call_target="tpu_custom_call" | custom-call | tf_op jit(solution)/shard_map/pack/pallas_call | solution.py:146
  2.6 5.0 %collective-permute-start.4 = (bf16[18,96,128]{2,1,0:T(8,128)(2,1)}, bf16[18,96,128]{2,1,0:T(8,128)(2,1)S(1)}, u32[]{:S(2)}, u32[]{:S(2)}) collective-permute-start(bf16[18,96,128]{2,1,0:T(8,128)(2,1)} %pack.15), channel_id=1, source_target_pairs={{0,3},{1,0},{2,1},{3,2},{4,7},{5,4},{6,5},{7,6},{8,11},{9,8},{10,9... | collective-permute-start | bytes 1327112 | tf_op jit(solution)/shard_map/ppermute | solution.py:382
  7.7 2.7 %pack.11 = bf16[18,96,128]{2,1,0:T(8,128)(2,1)} custom-call(s32[1]{0:T(128)} %bitcast.place, bf16[96,16,1024]{2,1,0:T(8,128)(2,1)} %refs_1_.7, bf16[96,16,1024]{2,1,0:T(8,128)(2,1)} %refs_1_.7, bf16[96,16,1024]{2,1,0:T(8,128)(2,1)} %refs_1_.7), custom_call_target="tpu_custom_call" | custom-call | tf_op jit(solution)/shard_map/pack/pallas_call | solution.py:146
  10.4 2.7 %pack.13 = bf16[18,96,128]{2,1,0:T(8,128)(2,1)} custom-call(s32[1]{0:T(128)} %bitcast.place, bf16[96,16,1024]{2,1,0:T(8,128)(2,1)} %refs_1_.7, bf16[96,16,1024]{2,1,0:T(8,128)(2,1)} %refs_1_.7, bf16[96,16,1024]{2,1,0:T(8,128)(2,1)} %refs_1_.7), custom_call_target="tpu_custom_call" | custom-call | tf_op jit(solution)/shard_map/pack/pallas_call | solution.py:146
  14.1 2.5 %pack.12 = bf16[17,96,128]{2,1,0:T(8,128)(2,1)} custom-call(s32[1]{0:T(128)} %bitcast.place, bf16[96,16,1024]{2,1,0:T(8,128)(2,1)} %refs_1_.7, bf16[96,16,1024]{2,1,0:T(8,128)(2,1)} %refs_1_.7), custom_call_target="tpu_custom_call" | custom-call | tf_op jit(solution)/shard_map/pack/pallas_call | solution.py:146
  16.6 2.5 %pack.10 = bf16[17,96,128]{2,1,0:T(8,128)(2,1)} custom-call(s32[1]{0:T(128)} %bitcast.place, bf16[96,16,1024]{2,1,0:T(8,128)(2,1)} %refs_1_.7, bf16[96,16,1024]{2,1,0:T(8,128)(2,1)} %refs_1_.7), custom_call_target="tpu_custom_call" | custom-call | tf_op jit(solution)/shard_map/pack/pallas_call | solution.py:146
  19.1 2.5 %pack.8.refs_0_ = bf16[17,96,128]{2,1,0:T(8,128)(2,1)} custom-call(s32[1]{0:T(128)} %bitcast.place, bf16[96,16,1024]{2,1,0:T(8,128)(2,1)} %refs_1_.7, bf16[96,16,1024]{2,1,0:T(8,128)(2,1)} %refs_1_.7), custom_call_target="tpu_custom_call" | custom-call | tf_op jit(solution)/shard_map/pack/pallas_call | solution.py:146
  21.6 2.5 %pack.14 = bf16[17,96,128]{2,1,0:T(8,128)(2,1)} custom-call(s32[1]{0:T(128)} %bitcast.place, bf16[96,16,1024]{2,1,0:T(8,128)(2,1)} %refs_1_.7, bf16[96,16,1024]{2,1,0:T(8,128)(2,1)} %refs_1_.7), custom_call_target="tpu_custom_call" | custom-call | tf_op jit(solution)/shard_map/pack/pallas_call | solution.py:146
  24.0 2.7 %pack.9.refs_0_ = bf16[18,96,128]{2,1,0:T(8,128)(2,1)} custom-call(s32[1]{0:T(128)} %bitcast.place, bf16[96,16,1024]{2,1,0:T(8,128)(2,1)} %refs_1_.7, bf16[96,16,1024]{2,1,0:T(8,128)(2,1)} %refs_1_.7, bf16[96,16,1024]{2,1,0:T(8,128)(2,1)} %refs_1_.7), custom_call_target="tpu_custom_call" | custom-call | tf_op jit(solution)/shard_map/pack/pallas_call | solution.py:146
  29.0 16.6 %collective-permute-done.2.refs_2_ = bf16[18,96,128]{2,1,0:T(8,128)(2,1)S(1)} collective-permute-done((bf16[18,96,128]{2,1,0:T(8,128)(2,1)}, bf16[18,96,128]{2,1,0:T(8,128)(2,1)S(1)}, u32[]{:S(2)}, u32[]{:S(2)}) %collective-permute-start.2) | collective-permute-done | bytes 442400 | tf_op jit(solution)/shard_map/ppermute | solution.py:382
  45.9 2.7 %collective-permute-start.7 = (bf16[7,384,128]{2,1,0:T(8,128)(2,1)S(1)}, bf16[7,384,128]{2,1,0:T(8,128)(2,1)S(1)}, u32[]{:S(2)}, u32[]{:S(2)}) collective-permute-start(bf16[7,384,128]{2,1,0:T(8,128)(2,1)S(1)} %pad_maximum_fusion.1), channel_id=1, source_target_pairs={{4,0},{8,4},{12,8},{16,12},{20,16},{24,20},{28,24},{0,28},{5,1},{9... | collective-permute-start | bytes 2064392 | tf_op jit(solution)/shard_map/ppermute | solution.py:408
  50.0 4.4 %collective-permute-start.5 = (bf16[17,96,128]{2,1,0:T(8,128)(2,1)S(1)}, bf16[17,96,128]{2,1,0:T(8,128)(2,1)S(1)}, u32[]{:S(2)}, u32[]{:S(2)}) collective-permute-start(bf16[17,96,128]{2,1,0:T(8,128)(2,1)S(1)} %copy-done.2), channel_id=1, source_target_pairs={{0,3},{1,0},{2,1},{3,2},{4,7},{5,4},{6,5},{7,6},{8,11},{9,8},{10,9... | collective-permute-start | bytes 1253384 | tf_op jit(solution)/shard_map/ppermute | solution.py:382
  55.1 7.4 %collective-permute-done.6.refs_4_ = bf16[7,384,128]{2,1,0:T(8,128)(2,1)S(1)} collective-permute-done((bf16[7,384,128]{2,1,0:T(8,128)(2,1)S(1)}, bf16[7,384,128]{2,1,0:T(8,128)(2,1)S(1)}, u32[]{:S(2)}, u32[]{:S(2)}) %collective-permute-start.6) | collective-permute-done | bytes 688160 | tf_op jit(solution)/shard_map/ppermute | solution.py:407
  62.5 18.6 %three_steps.2 = (bf16[16,96,128]{2,1,0:T(8,128)(2,1)S(1)}, bf16[16,96,128]{2,1,0:T(8,128)(2,1)S(1)}, bf16[16,96,128]{2,1,0:T(8,128)(2,1)S(1)}, bf16[16,96,128]{2,1,0:T(8,128)(2,1)S(1)}, f32[28,3,8,128]{3,2,1,0:T(8,128)S(1)}) custom-call(bf16[18,96,128]{2,1,0:T(8,128)(2,1)S(1)} %copy-done, bf16[18,96,128]{2,1,0:T(8,128)(2,1)S(1)} %collective-permute-done.refs_1_, ...), custom_call_target="tpu_custom_call" | custom-call | flops 6341787648 | bytes 8388608 | tf_op jit(solution)/shard_map/three_steps/pallas_call | solution.py:329
  81.2 7.3 %collective-permute-done.3.refs_2_ = bf16[17,96,128]{2,1,0:T(8,128)(2,1)S(1)} collective-permute-done((bf16[17,96,128]{2,1,0:T(8,128)(2,1)S(1)}, bf16[17,96,128]{2,1,0:T(8,128)(2,1)S(1)}, u32[]{:S(2)}, u32[]{:S(2)}) %collective-permute-start.3) | collective-permute-done | bytes 417824 | tf_op jit(solution)/shard_map/ppermute | solution.py:382
  89.6 2.7 %collective-permute-start.13 = (bf16[16,96,128]{2,1,0:T(8,128)(2,1)S(1)}, bf16[16,96,128]{2,1,0:T(8,128)(2,1)S(1)}, u32[]{:S(2)}, u32[]{:S(2)}) collective-permute-start(bf16[16,96,128]{2,1,0:T(8,128)(2,1)S(1)} %get-tuple-element.27), channel_id=1, source_target_pairs={{0,3},{1,0},{2,1},{3,2},{4,7},{5,4},{6,5},{7,6},{8,11},{9,8},{10,9... | collective-permute-start | bytes 1179656 | tf_op jit(solution)/shard_map/ppermute | solution.py:382
  92.9 9.9 %collective-permute-done.9.refs_5_ = bf16[7,384,128]{2,1,0:T(8,128)(2,1)S(1)} collective-permute-done((bf16[7,384,128]{2,1,0:T(8,128)(2,1)S(1)}, bf16[7,384,128]{2,1,0:T(8,128)(2,1)S(1)}, u32[]{:S(2)}, u32[]{:S(2)}) %collective-permute-start.9) | collective-permute-done | bytes 688160 | tf_op jit(solution)/shard_map/ppermute | solution.py:408
  102.8 3.7 %collective-permute-done.8.refs_4_ = bf16[7,384,128]{2,1,0:T(8,128)(2,1)S(1)} collective-permute-done((bf16[7,384,128]{2,1,0:T(8,128)(2,1)S(1)}, bf16[7,384,128]{2,1,0:T(8,128)(2,1)S(1)}, u32[]{:S(2)}, u32[]{:S(2)}) %collective-permute-start.8) | collective-permute-done | bytes 688160 | tf_op jit(solution)/shard_map/ppermute | solution.py:407
  106.5 18.6 %three_steps.3 = (bf16[16,96,128]{2,1,0:T(8,128)(2,1)S(1)}, bf16[16,96,128]{2,1,0:T(8,128)(2,1)S(1)}, bf16[16,96,128]{2,1,0:T(8,128)(2,1)S(1)}, bf16[16,96,128]{2,1,0:T(8,128)(2,1)S(1)}) custom-call(bf16[17,96,128]{2,1,0:T(8,128)(2,1)S(1)} %copy-done.1, bf16[17,96,128]{2,1,0:T(8,128)(2,1)S(1)} %collective-permute-done.1.refs_1_, ...), custom_call_target="tpu_custom_call" | custom-call | flops 6341787648 | bytes 8388608 | tf_op jit(solution)/shard_map/three_steps/pallas_call | solution.py:329
  125.0 2.7 %collective-permute-start.10 = (bf16[16,96,128]{2,1,0:T(8,128)(2,1)S(1)}, bf16[16,96,128]{2,1,0:T(8,128)(2,1)S(1)}, u32[]{:S(2)}, u32[]{:S(2)}) collective-permute-start(bf16[16,96,128]{2,1,0:T(8,128)(2,1)S(1)} %get-tuple-element.36), channel_id=1, source_target_pairs={{0,3},{1,0},{2,1},{3,2},{4,7},{5,4},{6,5},{7,6},{8,11},{9,8},{10,9... | collective-permute-start | bytes 1179656 | tf_op jit(solution)/shard_map/ppermute | solution.py:382
  128.4 2.7 %unpack.2.refs_4_ = bf16[96,16,1024]{2,1,0:T(8,128)(2,1)} custom-call(s32[1]{0:T(128)} %bitcast.place, bf16[16,96,128]{2,1,0:T(8,128)(2,1)S(1)} %get-tuple-element.26.refs_0_, bf16[16,96,128]{2,1,0:T(8,128)(2,1)S(1)} %collective-permute-done.13.refs_1_, bf16[16,96,128]{2,1,0:T(8,128)(2,1)S(1)} %collective-permute-done.14.refs_2_, ...), custom_call_target="tpu_custom_call" | custom-call | tf_op jit(solution)/shard_map/unpack/pallas_call | solution.py:185
  131.1 6.3 %collective-permute-done.10.refs_1_ = bf16[16,96,128]{2,1,0:T(8,128)(2,1)S(1)} collective-permute-done((bf16[16,96,128]{2,1,0:T(8,128)(2,1)S(1)}, bf16[16,96,128]{2,1,0:T(8,128)(2,1)S(1)}, u32[]{:S(2)}, u32[]{:S(2)}) %collective-permute-start.10) | collective-permute-done | bytes 393248 | tf_op jit(solution)/shard_map/ppermute | solution.py:382
  137.4 22.5 %collective-permute-done.11.refs_2_ = bf16[16,96,128]{2,1,0:T(8,128)(2,1)S(1)} collective-permute-done((bf16[16,96,128]{2,1,0:T(8,128)(2,1)S(1)}, bf16[16,96,128]{2,1,0:T(8,128)(2,1)S(1)}, u32[]{:S(2)}, u32[]{:S(2)}) %collective-permute-start.11) | collective-permute-done | bytes 393248 | tf_op jit(solution)/shard_map/ppermute | solution.py:382
  159.9 2.7 %unpack.3 = bf16[96,16,1024]{2,1,0:T(8,128)(2,1)} custom-call(s32[1]{0:T(128)} %bitcast.place, bf16[16,96,128]{2,1,0:T(8,128)(2,1)S(1)} %get-tuple-element.35.refs_0_, bf16[16,96,128]{2,1,0:T(8,128)(2,1)S(1)} %collective-permute-done.10.refs_1_, bf16[16,96,128]{2,1,0:T(8,128)(2,1)S(1)} %collective-permute-done.11.refs_2_, ...), custom_call_target="tpu_custom_call", output_to_operand_aliasing={{}: (5, {})} | custom-call | tf_op jit(solution)/shard_map/unpack/pallas_call | solution.py:185
  (86 shorter events, 7.9 us)
Async XLA Ops:
  2.6 26.3 %collective-permute-start.4 = (bf16[18,96,128]{2,1,0:T(8,128)(2,1)}, bf16[18,96,128]{2,1,0:T(8,128)(2,1)S(1)}, u32[]{:S(2)}, u32[]{:S(2)}) collective-permute-start(bf16[18,96,128]{2,1,0:T(8,128)(2,1)} %pack.15), channel_id=1, source_target_pairs={{0,3},{1,0},{2,1},{3,2},{4,7},{5,4},{6,5},{7,6},{8,11},{9,8},{10,9... | collective-permute-start | bytes 1327112 | tf_op jit(solution)/shard_map/ppermute | solution.py:382
  10.4 3.7 %copy-start.6 = (s32[384,6]{0,1:T(8,128)S(1)}, s32[384,6]{0,1:T(8,128)}, u32[]{:S(2)}) copy-start(s32[384,6]{0,1:T(8,128)} %param.9) | copy-start | bytes 27652
  10.4 18.6 %collective-permute-start = (bf16[18,96,128]{2,1,0:T(8,128)(2,1)}, bf16[18,96,128]{2,1,0:T(8,128)(2,1)S(1)}, u32[]{:S(2)}, u32[]{:S(2)}) collective-permute-start(bf16[18,96,128]{2,1,0:T(8,128)(2,1)} %pack.11), channel_id=1, source_target_pairs={{0,1},{1,2},{2,3},{3,0},{4,5},{5,6},{6,7},{7,4},{8,9},{9,10},{10,1... | collective-permute-start | bytes 1327112 | tf_op jit(solution)/shard_map/ppermute | solution.py:382
  13.1 32.6 %collective-permute-start.2 = (bf16[18,96,128]{2,1,0:T(8,128)(2,1)}, bf16[18,96,128]{2,1,0:T(8,128)(2,1)S(1)}, u32[]{:S(2)}, u32[]{:S(2)}) collective-permute-start(bf16[18,96,128]{2,1,0:T(8,128)(2,1)} %pack.13), channel_id=1, source_target_pairs={{0,2},{1,3},{2,0},{3,1},{4,6},{5,7},{6,4},{7,5},{8,10},{9,11},{10,... | collective-permute-start | bytes 1327112 | tf_op jit(solution)/shard_map/ppermute | solution.py:382
  24.0 2.9 %copy-start.9 = (f32[2,384]{1,0:T(2,128)S(1)}, f32[2,384]{1,0:T(2,128)}, u32[]{:S(2)}) copy-start(f32[2,384]{1,0:T(2,128)} %param.11) | copy-start | bytes 9220
  24.0 3.1 %copy-start.5 = (bf16[384,384]{1,0:T(8,128)(2,1)S(1)}, bf16[384,384]{1,0:T(8,128)(2,1)}, u32[]{:S(2)}) copy-start(bf16[384,384]{1,0:T(8,128)(2,1)} %param.7) | copy-start | bytes 884740
  24.0 3.7 %copy-start.7 = (s32[384,6]{0,1:T(8,128)S(1)}, s32[384,6]{0,1:T(8,128)}, u32[]{:S(2)}) copy-start(s32[384,6]{0,1:T(8,128)} %param.8) | copy-start | bytes 27652
  45.8 16.7 %collective-permute-start.6 = (bf16[7,384,128]{2,1,0:T(8,128)(2,1)S(1)}, bf16[7,384,128]{2,1,0:T(8,128)(2,1)S(1)}, u32[]{:S(2)}, u32[]{:S(2)}) collective-permute-start(bf16[7,384,128]{2,1,0:T(8,128)(2,1)S(1)} %pad_maximum_fusion), channel_id=1, source_target_pairs={{0,4},{4,8},{8,12},{12,16},{16,20},{20,24},{24,28},{28,0},{1,5},{5... | collective-permute-start | bytes 2064392 | tf_op jit(solution)/shard_map/ppermute | solution.py:407
  45.9 16.7 %collective-permute-start.7 = (bf16[7,384,128]{2,1,0:T(8,128)(2,1)S(1)}, bf16[7,384,128]{2,1,0:T(8,128)(2,1)S(1)}, u32[]{:S(2)}, u32[]{:S(2)}) collective-permute-start(bf16[7,384,128]{2,1,0:T(8,128)(2,1)S(1)} %pad_maximum_fusion.1), channel_id=1, source_target_pairs={{4,0},{8,4},{12,8},{16,12},{20,16},{24,20},{28,24},{0,28},{5,1},{9... | collective-permute-start | bytes 2064392 | tf_op jit(solution)/shard_map/ppermute | solution.py:408
  49.0 5.4 %copy-start.4 = (bf16[17,96,128]{2,1,0:T(8,128)(2,1)S(1)}, bf16[17,96,128]{2,1,0:T(8,128)(2,1)}, u32[]{:S(2)}) copy-start(bf16[17,96,128]{2,1,0:T(8,128)(2,1)} %pack.10) | copy-start | bytes 1253380
  49.0 5.4 %copy-start.3 = (bf16[17,96,128]{2,1,0:T(8,128)(2,1)S(1)}, bf16[17,96,128]{2,1,0:T(8,128)(2,1)}, u32[]{:S(2)}) copy-start(bf16[17,96,128]{2,1,0:T(8,128)(2,1)} %pack.12) | copy-start | bytes 1253380
  50.0 38.5 %collective-permute-start.5 = (bf16[17,96,128]{2,1,0:T(8,128)(2,1)S(1)}, bf16[17,96,128]{2,1,0:T(8,128)(2,1)S(1)}, u32[]{:S(2)}, u32[]{:S(2)}) collective-permute-start(bf16[17,96,128]{2,1,0:T(8,128)(2,1)S(1)} %copy-done.2), channel_id=1, source_target_pairs={{0,3},{1,0},{2,1},{3,2},{4,7},{5,4},{6,5},{7,6},{8,11},{9,8},{10,9... | collective-permute-start | bytes 1253384 | tf_op jit(solution)/shard_map/ppermute | solution.py:382
  54.4 26.8 %collective-permute-start.1 = (bf16[17,96,128]{2,1,0:T(8,128)(2,1)S(1)}, bf16[17,96,128]{2,1,0:T(8,128)(2,1)S(1)}, u32[]{:S(2)}, u32[]{:S(2)}) collective-permute-start(bf16[17,96,128]{2,1,0:T(8,128)(2,1)S(1)} %copy-done.4), channel_id=1, source_target_pairs={{0,1},{1,2},{2,3},{3,0},{4,5},{5,6},{6,7},{7,4},{8,9},{9,10},{10,1... | collective-permute-start | bytes 1253384 | tf_op jit(solution)/shard_map/ppermute | solution.py:382
  54.4 34.1 %collective-permute-start.3 = (bf16[17,96,128]{2,1,0:T(8,128)(2,1)S(1)}, bf16[17,96,128]{2,1,0:T(8,128)(2,1)S(1)}, u32[]{:S(2)}, u32[]{:S(2)}) collective-permute-start(bf16[17,96,128]{2,1,0:T(8,128)(2,1)S(1)} %copy-done.3), channel_id=1, source_target_pairs={{0,2},{1,3},{2,0},{3,1},{4,6},{5,7},{6,4},{7,5},{8,10},{9,11},{10,... | collective-permute-start | bytes 1253384 | tf_op jit(solution)/shard_map/ppermute | solution.py:382
  81.2 7.5 %slice-start.2 = ((bf16[17,96,128]{2,1,0:T(8,128)(2,1)}), bf16[7,96,128]{2,1,0:T(8,128)(2,1)S(1)}, s32[]{:S(2)}) async-start(bf16[17,96,128]{2,1,0:T(8,128)(2,1)} %pack.8.refs_0_), calls=%async_computation.2 | async-start | bytes 344064 | tf_op jit(solution)/shard_map/slice | solution.py:400
  88.6 17.8 %copy-start.1 = (bf16[17,96,128]{2,1,0:T(8,128)(2,1)S(1)}, bf16[17,96,128]{2,1,0:T(8,128)(2,1)}, u32[]{:S(2)}) copy-start(bf16[17,96,128]{2,1,0:T(8,128)(2,1)} %pack.8.refs_0_) | copy-start | bytes 1253380
  88.7 14.1 %collective-permute-start.9 = (bf16[7,384,128]{2,1,0:T(8,128)(2,1)S(1)}, bf16[7,384,128]{2,1,0:T(8,128)(2,1)S(1)}, u32[]{:S(2)}, u32[]{:S(2)}) collective-permute-start(bf16[7,384,128]{2,1,0:T(8,128)(2,1)S(1)} %pad_maximum_fusion.2), channel_id=1, source_target_pairs={{4,0},{8,4},{12,8},{16,12},{20,16},{24,20},{28,24},{0,28},{5,1},{9... | collective-permute-start | bytes 2064392 | tf_op jit(solution)/shard_map/ppermute | solution.py:408
  89.5 17.0 %collective-permute-start.8 = (bf16[7,384,128]{2,1,0:T(8,128)(2,1)S(1)}, bf16[7,384,128]{2,1,0:T(8,128)(2,1)S(1)}, u32[]{:S(2)}, u32[]{:S(2)}) collective-permute-start(bf16[7,384,128]{2,1,0:T(8,128)(2,1)S(1)} %maximum_maximum_fusion), channel_id=1, source_target_pairs={{0,4},{4,8},{8,12},{12,16},{16,20},{20,24},{24,28},{28,0},{1,5},{5... | collective-permute-start | bytes 2064392 | tf_op jit(solution)/shard_map/ppermute | solution.py:407
  89.6 38.2 %collective-permute-start.13 = (bf16[16,96,128]{2,1,0:T(8,128)(2,1)S(1)}, bf16[16,96,128]{2,1,0:T(8,128)(2,1)S(1)}, u32[]{:S(2)}, u32[]{:S(2)}) collective-permute-start(bf16[16,96,128]{2,1,0:T(8,128)(2,1)S(1)} %get-tuple-element.27), channel_id=1, source_target_pairs={{0,3},{1,0},{2,1},{3,2},{4,7},{5,4},{6,5},{7,6},{8,11},{9,8},{10,9... | collective-permute-start | bytes 1179656 | tf_op jit(solution)/shard_map/ppermute | solution.py:382
  92.3 36.1 %collective-permute-start.14 = (bf16[16,96,128]{2,1,0:T(8,128)(2,1)S(1)}, bf16[16,96,128]{2,1,0:T(8,128)(2,1)S(1)}, u32[]{:S(2)}, u32[]{:S(2)}) collective-permute-start(bf16[16,96,128]{2,1,0:T(8,128)(2,1)S(1)} %get-tuple-element.28), channel_id=1, source_target_pairs={{0,2},{1,3},{2,0},{3,1},{4,6},{5,7},{6,4},{7,5},{8,10},{9,11},{10,... | collective-permute-start | bytes 1179656 | tf_op jit(solution)/shard_map/ppermute | solution.py:382
  92.3 36.1 %collective-permute-start.15 = (bf16[16,96,128]{2,1,0:T(8,128)(2,1)S(1)}, bf16[16,96,128]{2,1,0:T(8,128)(2,1)S(1)}, u32[]{:S(2)}, u32[]{:S(2)}) collective-permute-start(bf16[16,96,128]{2,1,0:T(8,128)(2,1)S(1)} %get-tuple-element.29), channel_id=1, source_target_pairs={{0,1},{1,2},{2,3},{3,0},{4,5},{5,6},{6,7},{7,4},{8,9},{9,10},{10,1... | collective-permute-start | bytes 1179656 | tf_op jit(solution)/shard_map/ppermute | solution.py:382
  125.0 12.3 %collective-permute-start.10 = (bf16[16,96,128]{2,1,0:T(8,128)(2,1)S(1)}, bf16[16,96,128]{2,1,0:T(8,128)(2,1)S(1)}, u32[]{:S(2)}, u32[]{:S(2)}) collective-permute-start(bf16[16,96,128]{2,1,0:T(8,128)(2,1)S(1)} %get-tuple-element.36), channel_id=1, source_target_pairs={{0,3},{1,0},{2,1},{3,2},{4,7},{5,4},{6,5},{7,6},{8,11},{9,8},{10,9... | collective-permute-start | bytes 1179656 | tf_op jit(solution)/shard_map/ppermute | solution.py:382
  127.7 32.1 %collective-permute-start.11 = (bf16[16,96,128]{2,1,0:T(8,128)(2,1)S(1)}, bf16[16,96,128]{2,1,0:T(8,128)(2,1)S(1)}, u32[]{:S(2)}, u32[]{:S(2)}) collective-permute-start(bf16[16,96,128]{2,1,0:T(8,128)(2,1)S(1)} %get-tuple-element.37), channel_id=1, source_target_pairs={{0,2},{1,3},{2,0},{3,1},{4,6},{5,7},{6,4},{7,5},{8,10},{9,11},{10,... | collective-permute-start | bytes 1179656 | tf_op jit(solution)/shard_map/ppermute | solution.py:382
  127.8 32.1 %collective-permute-start.12 = (bf16[16,96,128]{2,1,0:T(8,128)(2,1)S(1)}, bf16[16,96,128]{2,1,0:T(8,128)(2,1)S(1)}, u32[]{:S(2)}, u32[]{:S(2)}) collective-permute-start(bf16[16,96,128]{2,1,0:T(8,128)(2,1)S(1)} %get-tuple-element.38), channel_id=1, source_target_pairs={{0,1},{1,2},{2,3},{3,0},{4,5},{5,6},{6,7},{7,4},{8,9},{9,10},{10,1... | collective-permute-start | bytes 1179656 | tf_op jit(solution)/shard_map/ppermute | solution.py:382
  (5 other events, 6.6 us)

commit v2 on v1

--- a/solution.py
+++ b/solution.py
@@ -100,6 +100,7 @@
 REACH = 2 * TIME_STEPS
 GROUP = 8
 SLOT = LANES // GROUP
+TOGETHER = 4
 
 
 def pack_kernel(place, main_ref, *refs):
@@ -206,7 +207,8 @@
     edge_in, refs = (refs[5], refs[6:]) if joined else (None, refs[5:])
     outs, refs = refs[:devices], refs[devices:]
     edge_out, refs = (refs[0], refs[1:]) if followed else (None, refs)
-    buffers, waiting = refs[:2], refs[2:]
+    buffers, waiting = refs[:2], refs[2]
+    together = waiting.shape[1] // (LANES + 2 * GROUP)
     share = blocks[0].shape[1]
     number = share * devices
     rows = outs[0].shape[0]
@@ -262,7 +264,7 @@
             keep, by_row, by_column, row_sign, column_sign = (coefficients[k : k + 1, lanes] for k in range(5))
             forward_row = jnp.broadcast_to(row_sign, (length, LANES)) > 0
             forward_column = jnp.broadcast_to(column_sign, (length, LANES)) > 0
-            for half in range(2):
+            for half in range(together):
 
                 def at(row, column):
                     return source[index + half + row, tile, start + column : start + column + length]
@@ -288,11 +290,12 @@
         source, target = buffers[step % 2], buffers[(step + 1) % 2]
         last = step == TIME_STEPS - 1
         start, length = (2 * GROUP, LANES) if last else (GROUP, LANES + 2 * GROUP)
-        low, pairs = 2 * (step + 1), rows // 2 + REACH - 2 * (step + 1)
+        low = 2 * (step + 1)
+        turns = (rows + 2 * REACH - 2 * low) // together
 
         def finish(slot, index):
-            result = rotate(waiting[slot][: 2 * length]).astype(jnp.float32)
-            for half in range(2):
+            result = rotate(waiting[slot, : together * length]).astype(jnp.float32)
+            for half in range(together):
                 cells = result[half * length : (half + 1) * length]
                 if last:
                     back = cells.T.astype(jnp.bfloat16)
@@ -304,15 +307,15 @@
                             :, tile * LANES : (tile + 1) * LANES
                         ]
 
-        advect(source, low, start, length, waiting[0])
-
-        @pl.loop(0, pairs // 2)
+        advect(source, low, start, length, waiting.at[0])
+
+        @pl.loop(0, turns)
         def _(turn_index):
-            index = low + 4 * turn_index
-            advect(source, index + 2, start, length, waiting[1])
-            finish(0, index)
-            advect(source, jnp.minimum(index + 4, low + 2 * pairs - 2), start, length, waiting[0])
-            finish(1, index + 2)
+            index = low + together * turn_index
+            slot = lax.rem(turn_index, 2)
+            following = jnp.minimum(index + together, low + together * (turns - 1))
+            advect(source, following, start, length, waiting.at[1 - slot])
+            finish(slot, index)
 
 
 def three_steps(blocks, above, below, kernel, turn, coefficients, rows, edge, followed):
@@ -333,7 +336,7 @@
         out_shape=out_shape,
         scratch_shapes=[
             *[pltpu.VMEM((tall, tiles, LANES + 4 * GROUP, LANES), jnp.float32)] * 2,
-            *[pltpu.VMEM((2 * (LANES + 2 * GROUP), number), jnp.bfloat16)] * 2,
+            pltpu.VMEM((2, TOGETHER * (LANES + 2 * GROUP), number), jnp.bfloat16),
         ],
         compiler_params=pltpu.CompilerParams(vmem_limit_bytes=48 * 2**20),
         cost_estimate=pl.CostEstimate(

time: 163 us -> 163 us (level)
  Pallas kernels: 63.2 us -> 59.2 us
  waiting for transfers between devices: 73.7 us -> 77.5 us
    pallas_call x2, Pallas kernels: 37.2 us -> 33.2 us  [three_steps(): pl.pallas_call(functools.partial(steps_kernel, devices, edge is not None,...]
    ppermute x12, waiting for transfers between devices: 52.7 us -> 56.5 us  [ahead(): lax.ppermute(value, 'ao', [(i, (i + shift) % devices) for i in range(devi...]
  transfers between devices with their start and end apart: 16 -> 16, of which waited for: 8 -> 8; matrix products, arithmetic and copies ran while one was open for 2% -> 2% of each run, Pallas kernels for 36% -> 33%
where the time goes in v2:
time: 163 us
  waiting for transfers between devices  77.5 us (48%)
  Pallas kernels  59.2 us (36%)
  starting transfers between devices  20.7 us (13%)
  local copies, waits for them, and re-layouts  2.83 us (2%)
  other arithmetic  1.74 us (1%)
    ppermute x12, waiting for transfers between devices, ahead(): lax.ppermute(value, 'ao', [(i, (i + shift) % devices) for i in range(devi...  56.5 us
    pallas_call x2, Pallas kernels, three_steps(): pl.pallas_call(functools.partial(steps_kernel, devices, edge is not None,...  33.2 us
    pallas_call x8, Pallas kernels, pack(): pl.pallas_call(pack_kernel, grid_spec=pltpu.PrefetchScalarGridSpec(num_sc...  20.7 us
    ppermute x12, starting transfers between devices, ahead(): lax.ppermute(value, 'ao', [(i, (i + shift) % devices) for i in range(devi...  17.8 us
    ppermute x2, waiting for transfers between devices, blocked(): above = lax.ppermute(upper, 'gx', up)  11.1 us
    ppermute x2, waiting for transfers between devices, blocked(): below = lax.ppermute(joint(0, REACH + 1), 'gx', down)  9.98 us
    pallas_call x2, Pallas kernels, unpack(): pl.pallas_call(functools.partial(unpack_kernel, devices, part, parts), in...  5.37 us
  transfers between devices with their start and end apart: 16, of which 8 were waited for; matrix products, arithmetic and copies ran while one was open for 2% of the time, Pallas kernels for 33%

profile of v2, /device:TPU:0, one launch (start us, length us, event | category | flops | bytes accessed | tf_op | source)
XLA Modules:
  0.0 162.6 jit_solution(3781425203217295171)
XLA Ops:
  0.0 2.6 %pack.15 = bf16[18,96,128]{2,1,0:T(8,128)(2,1)} custom-call(s32[1]{0:T(128)} %bitcast.place, bf16[96,16,1024]{2,1,0:T(8,128)(2,1)} %refs_1_.7, bf16[96,16,1024]{2,1,0:T(8,128)(2,1)} %refs_1_.7, bf16[96,16,1024]{2,1,0:T(8,128)(2,1)} %refs_1_.7), custom_call_target="tpu_custom_call" | custom-call | tf_op jit(solution)/shard_map/pack/pallas_call | solution.py:147
  2.6 5.0 %collective-permute-start.4 = (bf16[18,96,128]{2,1,0:T(8,128)(2,1)}, bf16[18,96,128]{2,1,0:T(8,128)(2,1)S(1)}, u32[]{:S(2)}, u32[]{:S(2)}) collective-permute-start(bf16[18,96,128]{2,1,0:T(8,128)(2,1)} %pack.15), channel_id=1, source_target_pairs={{0,3},{1,0},{2,1},{3,2},{4,7},{5,4},{6,5},{7,6},{8,11},{9,8},{10,9... | collective-permute-start | bytes 1327112 | tf_op jit(solution)/shard_map/ppermute | solution.py:385
  7.7 2.7 %pack.11 = bf16[18,96,128]{2,1,0:T(8,128)(2,1)} custom-call(s32[1]{0:T(128)} %bitcast.place, bf16[96,16,1024]{2,1,0:T(8,128)(2,1)} %refs_1_.7, bf16[96,16,1024]{2,1,0:T(8,128)(2,1)} %refs_1_.7, bf16[96,16,1024]{2,1,0:T(8,128)(2,1)} %refs_1_.7), custom_call_target="tpu_custom_call" | custom-call | tf_op jit(solution)/shard_map/pack/pallas_call | solution.py:147
  10.4 2.7 %pack.13 = bf16[18,96,128]{2,1,0:T(8,128)(2,1)} custom-call(s32[1]{0:T(128)} %bitcast.place, bf16[96,16,1024]{2,1,0:T(8,128)(2,1)} %refs_1_.7, bf16[96,16,1024]{2,1,0:T(8,128)(2,1)} %refs_1_.7, bf16[96,16,1024]{2,1,0:T(8,128)(2,1)} %refs_1_.7), custom_call_target="tpu_custom_call" | custom-call | tf_op jit(solution)/shard_map/pack/pallas_call | solution.py:147
  14.1 2.5 %pack.12 = bf16[17,96,128]{2,1,0:T(8,128)(2,1)} custom-call(s32[1]{0:T(128)} %bitcast.place, bf16[96,16,1024]{2,1,0:T(8,128)(2,1)} %refs_1_.7, bf16[96,16,1024]{2,1,0:T(8,128)(2,1)} %refs_1_.7), custom_call_target="tpu_custom_call" | custom-call | tf_op jit(solution)/shard_map/pack/pallas_call | solution.py:147
  16.6 2.5 %pack.10 = bf16[17,96,128]{2,1,0:T(8,128)(2,1)} custom-call(s32[1]{0:T(128)} %bitcast.place, bf16[96,16,1024]{2,1,0:T(8,128)(2,1)} %refs_1_.7, bf16[96,16,1024]{2,1,0:T(8,128)(2,1)} %refs_1_.7), custom_call_target="tpu_custom_call" | custom-call | tf_op jit(solution)/shard_map/pack/pallas_call | solution.py:147
  19.1 2.5 %pack.8.refs_0_ = bf16[17,96,128]{2,1,0:T(8,128)(2,1)} custom-call(s32[1]{0:T(128)} %bitcast.place, bf16[96,16,1024]{2,1,0:T(8,128)(2,1)} %refs_1_.7, bf16[96,16,1024]{2,1,0:T(8,128)(2,1)} %refs_1_.7), custom_call_target="tpu_custom_call" | custom-call | tf_op jit(solution)/shard_map/pack/pallas_call | solution.py:147
  21.6 2.5 %pack.14 = bf16[17,96,128]{2,1,0:T(8,128)(2,1)} custom-call(s32[1]{0:T(128)} %bitcast.place, bf16[96,16,1024]{2,1,0:T(8,128)(2,1)} %refs_1_.7, bf16[96,16,1024]{2,1,0:T(8,128)(2,1)} %refs_1_.7), custom_call_target="tpu_custom_call" | custom-call | tf_op jit(solution)/shard_map/pack/pallas_call | solution.py:147
  24.0 2.7 %pack.9.refs_0_ = bf16[18,96,128]{2,1,0:T(8,128)(2,1)} custom-call(s32[1]{0:T(128)} %bitcast.place, bf16[96,16,1024]{2,1,0:T(8,128)(2,1)} %refs_1_.7, bf16[96,16,1024]{2,1,0:T(8,128)(2,1)} %refs_1_.7, bf16[96,16,1024]{2,1,0:T(8,128)(2,1)} %refs_1_.7), custom_call_target="tpu_custom_call" | custom-call | tf_op jit(solution)/shard_map/pack/pallas_call | solution.py:147
  29.0 16.6 %collective-permute-done.2.refs_2_ = bf16[18,96,128]{2,1,0:T(8,128)(2,1)S(1)} collective-permute-done((bf16[18,96,128]{2,1,0:T(8,128)(2,1)}, bf16[18,96,128]{2,1,0:T(8,128)(2,1)S(1)}, u32[]{:S(2)}, u32[]{:S(2)}) %collective-permute-start.2) | collective-permute-done | bytes 442400 | tf_op jit(solution)/shard_map/ppermute | solution.py:385
  45.9 2.7 %collective-permute-start.7 = (bf16[7,384,128]{2,1,0:T(8,128)(2,1)S(1)}, bf16[7,384,128]{2,1,0:T(8,128)(2,1)S(1)}, u32[]{:S(2)}, u32[]{:S(2)}) collective-permute-start(bf16[7,384,128]{2,1,0:T(8,128)(2,1)S(1)} %pad_maximum_fusion.1), channel_id=1, source_target_pairs={{4,0},{8,4},{12,8},{16,12},{20,16},{24,20},{28,24},{0,28},{5,1},{9... | collective-permute-start | bytes 2064392 | tf_op jit(solution)/shard_map/ppermute | solution.py:411
  50.0 4.4 %collective-permute-start.5 = (bf16[17,96,128]{2,1,0:T(8,128)(2,1)S(1)}, bf16[17,96,128]{2,1,0:T(8,128)(2,1)S(1)}, u32[]{:S(2)}, u32[]{:S(2)}) collective-permute-start(bf16[17,96,128]{2,1,0:T(8,128)(2,1)S(1)} %copy-done.2), channel_id=1, source_target_pairs={{0,3},{1,0},{2,1},{3,2},{4,7},{5,4},{6,5},{7,6},{8,11},{9,8},{10,9... | collective-permute-start | bytes 1253384 | tf_op jit(solution)/shard_map/ppermute | solution.py:385
  55.1 7.4 %collective-permute-done.6.refs_4_ = bf16[7,384,128]{2,1,0:T(8,128)(2,1)S(1)} collective-permute-done((bf16[7,384,128]{2,1,0:T(8,128)(2,1)S(1)}, bf16[7,384,128]{2,1,0:T(8,128)(2,1)S(1)}, u32[]{:S(2)}, u32[]{:S(2)}) %collective-permute-start.6) | collective-permute-done | bytes 688160 | tf_op jit(solution)/shard_map/ppermute | solution.py:410
  62.5 16.6 %three_steps.2 = (bf16[16,96,128]{2,1,0:T(8,128)(2,1)S(1)}, bf16[16,96,128]{2,1,0:T(8,128)(2,1)S(1)}, bf16[16,96,128]{2,1,0:T(8,128)(2,1)S(1)}, bf16[16,96,128]{2,1,0:T(8,128)(2,1)S(1)}, f32[28,3,8,128]{3,2,1,0:T(8,128)S(1)}) custom-call(bf16[18,96,128]{2,1,0:T(8,128)(2,1)S(1)} %copy-done, bf16[18,96,128]{2,1,0:T(8,128)(2,1)S(1)} %collective-permute-done.refs_1_, ...), custom_call_target="tpu_custom_call" | custom-call | flops 6341787648 | bytes 8388608 | tf_op jit(solution)/shard_map/three_steps/pallas_call | solution.py:332
  79.2 9.2 %collective-permute-done.3.refs_2_ = bf16[17,96,128]{2,1,0:T(8,128)(2,1)S(1)} collective-permute-done((bf16[17,96,128]{2,1,0:T(8,128)(2,1)S(1)}, bf16[17,96,128]{2,1,0:T(8,128)(2,1)S(1)}, u32[]{:S(2)}, u32[]{:S(2)}) %collective-permute-start.3) | collective-permute-done | bytes 417824 | tf_op jit(solution)/shard_map/ppermute | solution.py:385
  89.6 2.7 %collective-permute-start.13 = (bf16[16,96,128]{2,1,0:T(8,128)(2,1)S(1)}, bf16[16,96,128]{2,1,0:T(8,128)(2,1)S(1)}, u32[]{:S(2)}, u32[]{:S(2)}) collective-permute-start(bf16[16,96,128]{2,1,0:T(8,128)(2,1)S(1)} %get-tuple-element.27), channel_id=1, source_target_pairs={{0,3},{1,0},{2,1},{3,2},{4,7},{5,4},{6,5},{7,6},{8,11},{9,8},{10,9... | collective-permute-start | bytes 1179656 | tf_op jit(solution)/shard_map/ppermute | solution.py:385
  92.9 9.9 %collective-permute-done.9.refs_5_ = bf16[7,384,128]{2,1,0:T(8,128)(2,1)S(1)} collective-permute-done((bf16[7,384,128]{2,1,0:T(8,128)(2,1)S(1)}, bf16[7,384,128]{2,1,0:T(8,128)(2,1)S(1)}, u32[]{:S(2)}, u32[]{:S(2)}) %collective-permute-start.9) | collective-permute-done | bytes 688160 | tf_op jit(solution)/shard_map/ppermute | solution.py:411
  102.8 3.7 %collective-permute-done.8.refs_4_ = bf16[7,384,128]{2,1,0:T(8,128)(2,1)S(1)} collective-permute-done((bf16[7,384,128]{2,1,0:T(8,128)(2,1)S(1)}, bf16[7,384,128]{2,1,0:T(8,128)(2,1)S(1)}, u32[]{:S(2)}, u32[]{:S(2)}) %collective-permute-start.8) | collective-permute-done | bytes 688160 | tf_op jit(solution)/shard_map/ppermute | solution.py:410
  106.5 16.6 %three_steps.3 = (bf16[16,96,128]{2,1,0:T(8,128)(2,1)S(1)}, bf16[16,96,128]{2,1,0:T(8,128)(2,1)S(1)}, bf16[16,96,128]{2,1,0:T(8,128)(2,1)S(1)}, bf16[16,96,128]{2,1,0:T(8,128)(2,1)S(1)}) custom-call(bf16[17,96,128]{2,1,0:T(8,128)(2,1)S(1)} %copy-done.1, bf16[17,96,128]{2,1,0:T(8,128)(2,1)S(1)} %collective-permute-done.1.refs_1_, ...), custom_call_target="tpu_custom_call" | custom-call | flops 6341787648 | bytes 8388608 | tf_op jit(solution)/shard_map/three_steps/pallas_call | solution.py:332
  123.0 2.7 %collective-permute-start.10 = (bf16[16,96,128]{2,1,0:T(8,128)(2,1)S(1)}, bf16[16,96,128]{2,1,0:T(8,128)(2,1)S(1)}, u32[]{:S(2)}, u32[]{:S(2)}) collective-permute-start(bf16[16,96,128]{2,1,0:T(8,128)(2,1)S(1)} %get-tuple-element.36), channel_id=1, source_target_pairs={{0,3},{1,0},{2,1},{3,2},{4,7},{5,4},{6,5},{7,6},{8,11},{9,8},{10,9... | collective-permute-start | bytes 1179656 | tf_op jit(solution)/shard_map/ppermute | solution.py:385
  126.4 2.7 %unpack.2.refs_4_ = bf16[96,16,1024]{2,1,0:T(8,128)(2,1)} custom-call(s32[1]{0:T(128)} %bitcast.place, bf16[16,96,128]{2,1,0:T(8,128)(2,1)S(1)} %get-tuple-element.26.refs_0_, bf16[16,96,128]{2,1,0:T(8,128)(2,1)S(1)} %collective-permute-done.13.refs_1_, bf16[16,96,128]{2,1,0:T(8,128)(2,1)S(1)} %collective-permute-done.14.refs_2_, ...), custom_call_target="tpu_custom_call" | custom-call | tf_op jit(solution)/shard_map/unpack/pallas_call | solution.py:186
  129.1 6.3 %collective-permute-done.10.refs_1_ = bf16[16,96,128]{2,1,0:T(8,128)(2,1)S(1)} collective-permute-done((bf16[16,96,128]{2,1,0:T(8,128)(2,1)S(1)}, bf16[16,96,128]{2,1,0:T(8,128)(2,1)S(1)}, u32[]{:S(2)}, u32[]{:S(2)}) %collective-permute-start.10) | collective-permute-done | bytes 393248 | tf_op jit(solution)/shard_map/ppermute | solution.py:385
  135.4 24.3 %collective-permute-done.11.refs_2_ = bf16[16,96,128]{2,1,0:T(8,128)(2,1)S(1)} collective-permute-done((bf16[16,96,128]{2,1,0:T(8,128)(2,1)S(1)}, bf16[16,96,128]{2,1,0:T(8,128)(2,1)S(1)}, u32[]{:S(2)}, u32[]{:S(2)}) %collective-permute-start.11) | collective-permute-done | bytes 393248 | tf_op jit(solution)/shard_map/ppermute | solution.py:385
  159.7 2.7 %unpack.3 = bf16[96,16,1024]{2,1,0:T(8,128)(2,1)} custom-call(s32[1]{0:T(128)} %bitcast.place, bf16[16,96,128]{2,1,0:T(8,128)(2,1)S(1)} %get-tuple-element.35.refs_0_, bf16[16,96,128]{2,1,0:T(8,128)(2,1)S(1)} %collective-permute-done.10.refs_1_, bf16[16,96,128]{2,1,0:T(8,128)(2,1)S(1)} %collective-permute-done.11.refs_2_, ...), custom_call_target="tpu_custom_call", output_to_operand_aliasing={{}: (5, {})} | custom-call | tf_op jit(solution)/shard_map/unpack/pallas_call | solution.py:186
  (86 shorter events, 7.9 us)
Async XLA Ops:
  2.6 26.3 %collective-permute-start.4 = (bf16[18,96,128]{2,1,0:T(8,128)(2,1)}, bf16[18,96,128]{2,1,0:T(8,128)(2,1)S(1)}, u32[]{:S(2)}, u32[]{:S(2)}) collective-permute-start(bf16[18,96,128]{2,1,0:T(8,128)(2,1)} %pack.15), channel_id=1, source_target_pairs={{0,3},{1,0},{2,1},{3,2},{4,7},{5,4},{6,5},{7,6},{8,11},{9,8},{10,9... | collective-permute-start | bytes 1327112 | tf_op jit(solution)/shard_map/ppermute | solution.py:385
  10.4 3.7 %copy-start.6 = (s32[384,6]{0,1:T(8,128)S(1)}, s32[384,6]{0,1:T(8,128)}, u32[]{:S(2)}) copy-start(s32[384,6]{0,1:T(8,128)} %param.9) | copy-start | bytes 27652
  10.4 18.6 %collective-permute-start = (bf16[18,96,128]{2,1,0:T(8,128)(2,1)}, bf16[18,96,128]{2,1,0:T(8,128)(2,1)S(1)}, u32[]{:S(2)}, u32[]{:S(2)}) collective-permute-start(bf16[18,96,128]{2,1,0:T(8,128)(2,1)} %pack.11), channel_id=1, source_target_pairs={{0,1},{1,2},{2,3},{3,0},{4,5},{5,6},{6,7},{7,4},{8,9},{9,10},{10,1... | collective-permute-start | bytes 1327112 | tf_op jit(solution)/shard_map/ppermute | solution.py:385
  13.1 32.6 %collective-permute-start.2 = (bf16[18,96,128]{2,1,0:T(8,128)(2,1)}, bf16[18,96,128]{2,1,0:T(8,128)(2,1)S(1)}, u32[]{:S(2)}, u32[]{:S(2)}) collective-permute-start(bf16[18,96,128]{2,1,0:T(8,128)(2,1)} %pack.13), channel_id=1, source_target_pairs={{0,2},{1,3},{2,0},{3,1},{4,6},{5,7},{6,4},{7,5},{8,10},{9,11},{10,... | collective-permute-start | bytes 1327112 | tf_op jit(solution)/shard_map/ppermute | solution.py:385
  24.0 2.9 %copy-start.9 = (f32[2,384]{1,0:T(2,128)S(1)}, f32[2,384]{1,0:T(2,128)}, u32[]{:S(2)}) copy-start(f32[2,384]{1,0:T(2,128)} %param.11) | copy-start | bytes 9220
  24.0 3.1 %copy-start.5 = (bf16[384,384]{1,0:T(8,128)(2,1)S(1)}, bf16[384,384]{1,0:T(8,128)(2,1)}, u32[]{:S(2)}) copy-start(bf16[384,384]{1,0:T(8,128)(2,1)} %param.7) | copy-start | bytes 884740
  24.0 3.7 %copy-start.7 = (s32[384,6]{0,1:T(8,128)S(1)}, s32[384,6]{0,1:T(8,128)}, u32[]{:S(2)}) copy-start(s32[384,6]{0,1:T(8,128)} %param.8) | copy-start | bytes 27652
  45.8 16.7 %collective-permute-start.6 = (bf16[7,384,128]{2,1,0:T(8,128)(2,1)S(1)}, bf16[7,384,128]{2,1,0:T(8,128)(2,1)S(1)}, u32[]{:S(2)}, u32[]{:S(2)}) collective-permute-start(bf16[7,384,128]{2,1,0:T(8,128)(2,1)S(1)} %pad_maximum_fusion), channel_id=1, source_target_pairs={{0,4},{4,8},{8,12},{12,16},{16,20},{20,24},{24,28},{28,0},{1,5},{5... | collective-permute-start | bytes 2064392 | tf_op jit(solution)/shard_map/ppermute | solution.py:410
  45.9 16.7 %collective-permute-start.7 = (bf16[7,384,128]{2,1,0:T(8,128)(2,1)S(1)}, bf16[7,384,128]{2,1,0:T(8,128)(2,1)S(1)}, u32[]{:S(2)}, u32[]{:S(2)}) collective-permute-start(bf16[7,384,128]{2,1,0:T(8,128)(2,1)S(1)} %pad_maximum_fusion.1), channel_id=1, source_target_pairs={{4,0},{8,4},{12,8},{16,12},{20,16},{24,20},{28,24},{0,28},{5,1},{9... | collective-permute-start | bytes 2064392 | tf_op jit(solution)/shard_map/ppermute | solution.py:411
  49.0 5.4 %copy-start.4 = (bf16[17,96,128]{2,1,0:T(8,128)(2,1)S(1)}, bf16[17,96,128]{2,1,0:T(8,128)(2,1)}, u32[]{:S(2)}) copy-start(bf16[17,96,128]{2,1,0:T(8,128)(2,1)} %pack.10) | copy-start | bytes 1253380
  49.0 5.4 %copy-start.3 = (bf16[17,96,128]{2,1,0:T(8,128)(2,1)S(1)}, bf16[17,96,128]{2,1,0:T(8,128)(2,1)}, u32[]{:S(2)}) copy-start(bf16[17,96,128]{2,1,0:T(8,128)(2,1)} %pack.12) | copy-start | bytes 1253380
  50.0 38.5 %collective-permute-start.5 = (bf16[17,96,128]{2,1,0:T(8,128)(2,1)S(1)}, bf16[17,96,128]{2,1,0:T(8,128)(2,1)S(1)}, u32[]{:S(2)}, u32[]{:S(2)}) collective-permute-start(bf16[17,96,128]{2,1,0:T(8,128)(2,1)S(1)} %copy-done.2), channel_id=1, source_target_pairs={{0,3},{1,0},{2,1},{3,2},{4,7},{5,4},{6,5},{7,6},{8,11},{9,8},{10,9... | collective-permute-start | bytes 1253384 | tf_op jit(solution)/shard_map/ppermute | solution.py:385
  54.4 24.8 %collective-permute-start.1 = (bf16[17,96,128]{2,1,0:T(8,128)(2,1)S(1)}, bf16[17,96,128]{2,1,0:T(8,128)(2,1)S(1)}, u32[]{:S(2)}, u32[]{:S(2)}) collective-permute-start(bf16[17,96,128]{2,1,0:T(8,128)(2,1)S(1)} %copy-done.4), channel_id=1, source_target_pairs={{0,1},{1,2},{2,3},{3,0},{4,5},{5,6},{6,7},{7,4},{8,9},{9,10},{10,1... | collective-permute-start | bytes 1253384 | tf_op jit(solution)/shard_map/ppermute | solution.py:385
  54.4 34.1 %collective-permute-start.3 = (bf16[17,96,128]{2,1,0:T(8,128)(2,1)S(1)}, bf16[17,96,128]{2,1,0:T(8,128)(2,1)S(1)}, u32[]{:S(2)}, u32[]{:S(2)}) collective-permute-start(bf16[17,96,128]{2,1,0:T(8,128)(2,1)S(1)} %copy-done.3), channel_id=1, source_target_pairs={{0,2},{1,3},{2,0},{3,1},{4,6},{5,7},{6,4},{7,5},{8,10},{9,11},{10,... | collective-permute-start | bytes 1253384 | tf_op jit(solution)/shard_map/ppermute | solution.py:385
  79.2 9.4 %slice-start.2 = ((bf16[17,96,128]{2,1,0:T(8,128)(2,1)}), bf16[7,96,128]{2,1,0:T(8,128)(2,1)S(1)}, s32[]{:S(2)}) async-start(bf16[17,96,128]{2,1,0:T(8,128)(2,1)} %pack.8.refs_0_), calls=%async_computation.2 | async-start | bytes 344064 | tf_op jit(solution)/shard_map/slice | solution.py:403
  88.6 17.8 %copy-start.1 = (bf16[17,96,128]{2,1,0:T(8,128)(2,1)S(1)}, bf16[17,96,128]{2,1,0:T(8,128)(2,1)}, u32[]{:S(2)}) copy-start(bf16[17,96,128]{2,1,0:T(8,128)(2,1)} %pack.8.refs_0_) | copy-start | bytes 1253380
  88.7 14.1 %collective-permute-start.9 = (bf16[7,384,128]{2,1,0:T(8,128)(2,1)S(1)}, bf16[7,384,128]{2,1,0:T(8,128)(2,1)S(1)}, u32[]{:S(2)}, u32[]{:S(2)}) collective-permute-start(bf16[7,384,128]{2,1,0:T(8,128)(2,1)S(1)} %pad_maximum_fusion.2), channel_id=1, source_target_pairs={{4,0},{8,4},{12,8},{16,12},{20,16},{24,20},{28,24},{0,28},{5,1},{9... | collective-permute-start | bytes 2064392 | tf_op jit(solution)/shard_map/ppermute | solution.py:411
  89.5 17.0 %collective-permute-start.8 = (bf16[7,384,128]{2,1,0:T(8,128)(2,1)S(1)}, bf16[7,384,128]{2,1,0:T(8,128)(2,1)S(1)}, u32[]{:S(2)}, u32[]{:S(2)}) collective-permute-start(bf16[7,384,128]{2,1,0:T(8,128)(2,1)S(1)} %maximum_maximum_fusion), channel_id=1, source_target_pairs={{0,4},{4,8},{8,12},{12,16},{16,20},{20,24},{24,28},{28,0},{1,5},{5... | collective-permute-start | bytes 2064392 | tf_op jit(solution)/shard_map/ppermute | solution.py:410
  89.6 36.2 %collective-permute-start.13 = (bf16[16,96,128]{2,1,0:T(8,128)(2,1)S(1)}, bf16[16,96,128]{2,1,0:T(8,128)(2,1)S(1)}, u32[]{:S(2)}, u32[]{:S(2)}) collective-permute-start(bf16[16,96,128]{2,1,0:T(8,128)(2,1)S(1)} %get-tuple-element.27), channel_id=1, source_target_pairs={{0,3},{1,0},{2,1},{3,2},{4,7},{5,4},{6,5},{7,6},{8,11},{9,8},{10,9... | collective-permute-start | bytes 1179656 | tf_op jit(solution)/shard_map/ppermute | solution.py:385
  92.3 34.1 %collective-permute-start.14 = (bf16[16,96,128]{2,1,0:T(8,128)(2,1)S(1)}, bf16[16,96,128]{2,1,0:T(8,128)(2,1)S(1)}, u32[]{:S(2)}, u32[]{:S(2)}) collective-permute-start(bf16[16,96,128]{2,1,0:T(8,128)(2,1)S(1)} %get-tuple-element.28), channel_id=1, source_target_pairs={{0,2},{1,3},{2,0},{3,1},{4,6},{5,7},{6,4},{7,5},{8,10},{9,11},{10,... | collective-permute-start | bytes 1179656 | tf_op jit(solution)/shard_map/ppermute | solution.py:385
  92.3 34.1 %collective-permute-start.15 = (bf16[16,96,128]{2,1,0:T(8,128)(2,1)S(1)}, bf16[16,96,128]{2,1,0:T(8,128)(2,1)S(1)}, u32[]{:S(2)}, u32[]{:S(2)}) collective-permute-start(bf16[16,96,128]{2,1,0:T(8,128)(2,1)S(1)} %get-tuple-element.29), channel_id=1, source_target_pairs={{0,1},{1,2},{2,3},{3,0},{4,5},{5,6},{6,7},{7,4},{8,9},{9,10},{10,1... | collective-permute-start | bytes 1179656 | tf_op jit(solution)/shard_map/ppermute | solution.py:385
  123.0 12.3 %collective-permute-start.10 = (bf16[16,96,128]{2,1,0:T(8,128)(2,1)S(1)}, bf16[16,96,128]{2,1,0:T(8,128)(2,1)S(1)}, u32[]{:S(2)}, u32[]{:S(2)}) collective-permute-start(bf16[16,96,128]{2,1,0:T(8,128)(2,1)S(1)} %get-tuple-element.36), channel_id=1, source_target_pairs={{0,3},{1,0},{2,1},{3,2},{4,7},{5,4},{6,5},{7,6},{8,11},{9,8},{10,9... | collective-permute-start | bytes 1179656 | tf_op jit(solution)/shard_map/ppermute | solution.py:385
  125.7 34.0 %collective-permute-start.11 = (bf16[16,96,128]{2,1,0:T(8,128)(2,1)S(1)}, bf16[16,96,128]{2,1,0:T(8,128)(2,1)S(1)}, u32[]{:S(2)}, u32[]{:S(2)}) collective-permute-start(bf16[16,96,128]{2,1,0:T(8,128)(2,1)S(1)} %get-tuple-element.37), channel_id=1, source_target_pairs={{0,2},{1,3},{2,0},{3,1},{4,6},{5,7},{6,4},{7,5},{8,10},{9,11},{10,... | collective-permute-start | bytes 1179656 | tf_op jit(solution)/shard_map/ppermute | solution.py:385
  125.8 34.0 %collective-permute-start.12 = (bf16[16,96,128]{2,1,0:T(8,128)(2,1)S(1)}, bf16[16,96,128]{2,1,0:T(8,128)(2,1)S(1)}, u32[]{:S(2)}, u32[]{:S(2)}) collective-permute-start(bf16[16,96,128]{2,1,0:T(8,128)(2,1)S(1)} %get-tuple-element.38), channel_id=1, source_target_pairs={{0,1},{1,2},{2,3},{3,0},{4,5},{5,6},{6,7},{7,4},{8,9},{9,10},{10,1... | collective-permute-start | bytes 1179656 | tf_op jit(solution)/shard_map/ppermute | solution.py:385
  (5 other events, 6.6 us)

commit v3 on v2

--- a/solution.py
+++ b/solution.py
@@ -158,20 +158,20 @@
     )(place, *[density] * len(offsets))
 
 
-def unpack_kernel(devices, part, parts, place, *refs):
-    blocks, out_ref, wide, staged, sems = refs[:devices], *refs[-4:]
+def unpack_kernel(devices, shifts, part, parts, place, *refs):
+    blocks, out_ref, wide, staged, sems = refs[: len(shifts)], *refs[-4:]
     rows, share, _ = blocks[0].shape
     copies = []
-    for shift in range(devices):
-        wide[...] = blocks[shift][...].astype(jnp.float32).reshape(rows * share, LANES)
+    for number, shift in enumerate(shifts):
+        wide[...] = blocks[number][...].astype(jnp.float32).reshape(rows * share, LANES)
         for orient in range(share):
-            staged[shift, orient] = wide[pl.ds(orient, rows, stride=share), :].astype(jnp.bfloat16)
+            staged[number, orient] = wide[pl.ds(orient, rows, stride=share), :].astype(jnp.bfloat16)
         tile = lax.rem(place[0] + shift, devices) * parts + part
         copies.append(
             pltpu.make_async_copy(
-                staged.at[shift],
+                staged.at[number],
                 out_ref.at[:, :, pl.ds(pl.multiple_of(tile * LANES, LANES), LANES)],
-                sems.at[shift],
+                sems.at[number],
             )
         )
         copies[-1].start()
@@ -179,23 +179,24 @@
         copy.wait()
 
 
-def unpack(blocks, place, part, parts, shape, before):
+def unpack(blocks, shifts, place, part, parts, shape, before):
     devices = len(blocks)
+    blocks = [blocks[shift] for shift in shifts]
     rows, share, _ = blocks[0].shape
     earlier = () if before is None else (before,)
     return pl.pallas_call(
-        functools.partial(unpack_kernel, devices, part, parts),
+        functools.partial(unpack_kernel, devices, shifts, part, parts),
         in_specs=[pl.BlockSpec(memory_space=pltpu.SMEM)]
-        + [pl.BlockSpec(memory_space=pltpu.VMEM)] * devices
+        + [pl.BlockSpec(memory_space=pltpu.VMEM)] * len(shifts)
         + [pl.BlockSpec(memory_space=pl.ANY)] * len(earlier),
         out_specs=pl.BlockSpec(memory_space=pl.ANY),
         scratch_shapes=[
             pltpu.VMEM((rows * share, LANES), jnp.float32),
-            pltpu.VMEM((devices, share, rows, LANES), jnp.bfloat16),
-            pltpu.SemaphoreType.DMA((devices,)),
+            pltpu.VMEM((len(shifts), share, rows, LANES), jnp.bfloat16),
+            pltpu.SemaphoreType.DMA((len(shifts),)),
         ],
         out_shape=jax.ShapeDtypeStruct(shape, jnp.bfloat16),
-        input_output_aliases={1 + devices: 0} if earlier else {},
+        input_output_aliases={1 + len(shifts): 0} if earlier else {},
         compiler_params=pltpu.CompilerParams(vmem_limit_bytes=16 * 2**20),
         name="unpack",
     )(place, *blocks, *earlier)
@@ -417,7 +418,10 @@
     for part in range(parts):
         result = results[part]
         returned = [result[0]] + [ahead(result[shift], devices - shift) for shift in range(1, devices)]
-        evolved = unpack(returned, place, part, parts, density.shape, evolved)
+        middle = devices // 2 if part + 1 == parts else devices
+        for shifts in (range(middle), range(middle, devices)):
+            if len(shifts):
+                evolved = unpack(returned, shifts, place, part, parts, density.shape, evolved)
     return evolved
 
 

time: 163 us -> 162 us (level)
  waiting for transfers between devices: 77.5 us -> 75.8 us
    ppermute x12, waiting for transfers between devices: 56.5 us -> 54.8 us  [ahead(): lax.ppermute(value, 'ao', [(i, (i + shift) % devices) for i in range(devi...]
    pallas_call x2 -> x3, Pallas kernels: 5.37 us -> 6.12 us  [unpack(): pl.pallas_call(functools.partial(unpack_kernel, devices, shifts, part, pa...]
  transfers between devices with their start and end apart: 16 -> 16, of which waited for: 8 -> 8; matrix products, arithmetic and copies ran while one was open for 2% -> 2% of each run, Pallas kernels for 33% -> 34%
where the time goes in v3:
time: 162 us
  waiting for transfers between devices  75.8 us (47%)
  Pallas kernels  60 us (37%)
  starting transfers between devices  20.7 us (13%)
  local copies, waits for them, and re-layouts  2.83 us (2%)
  other arithmetic  1.74 us (1%)
    ppermute x12, waiting for transfers between devices, ahead(): lax.ppermute(value, 'ao', [(i, (i + shift) % devices) for i in range(devi...  54.8 us
    pallas_call x2, Pallas kernels, three_steps(): pl.pallas_call(functools.partial(steps_kernel, devices, edge is not None,...  33.2 us
    pallas_call x8, Pallas kernels, pack(): pl.pallas_call(pack_kernel, grid_spec=pltpu.PrefetchScalarGridSpec(num_sc...  20.7 us
    ppermute x12, starting transfers between devices, ahead(): lax.ppermute(value, 'ao', [(i, (i + shift) % devices) for i in range(devi...  17.8 us
    ppermute x2, waiting for transfers between devices, blocked(): above = lax.ppermute(upper, 'gx', up)  11.1 us
    ppermute x2, waiting for transfers between devices, blocked(): below = lax.ppermute(joint(0, REACH + 1), 'gx', down)  9.98 us
    pallas_call x3, Pallas kernels, unpack(): pl.pallas_call(functools.partial(unpack_kernel, devices, shifts, part, pa...  6.12 us
  transfers between devices with their start and end apart: 16, of which 8 were waited for; matrix products, arithmetic and copies ran while one was open for 2% of the time, Pallas kernels for 34%

profile of v3, /device:TPU:0, one launch (start us, length us, event | category | flops | bytes accessed | tf_op | source)
XLA Modules:
  0.0 161.6 jit_solution(5862321902936087550)
XLA Ops:
  0.0 2.6 %pack.15 = bf16[18,96,128]{2,1,0:T(8,128)(2,1)} custom-call(s32[1]{0:T(128)} %bitcast.place, bf16[96,16,1024]{2,1,0:T(8,128)(2,1)} %refs_1_.7, bf16[96,16,1024]{2,1,0:T(8,128)(2,1)} %refs_1_.7, bf16[96,16,1024]{2,1,0:T(8,128)(2,1)} %refs_1_.7), custom_call_target="tpu_custom_call" | custom-call | tf_op jit(solution)/shard_map/pack/pallas_call | solution.py:147
  2.6 5.0 %collective-permute-start.4 = (bf16[18,96,128]{2,1,0:T(8,128)(2,1)}, bf16[18,96,128]{2,1,0:T(8,128)(2,1)S(1)}, u32[]{:S(2)}, u32[]{:S(2)}) collective-permute-start(bf16[18,96,128]{2,1,0:T(8,128)(2,1)} %pack.15), channel_id=1, source_target_pairs={{0,3},{1,0},{2,1},{3,2},{4,7},{5,4},{6,5},{7,6},{8,11},{9,8},{10,9... | collective-permute-start | bytes 1327112 | tf_op jit(solution)/shard_map/ppermute | solution.py:386
  7.7 2.7 %pack.11 = bf16[18,96,128]{2,1,0:T(8,128)(2,1)} custom-call(s32[1]{0:T(128)} %bitcast.place, bf16[96,16,1024]{2,1,0:T(8,128)(2,1)} %refs_1_.7, bf16[96,16,1024]{2,1,0:T(8,128)(2,1)} %refs_1_.7, bf16[96,16,1024]{2,1,0:T(8,128)(2,1)} %refs_1_.7), custom_call_target="tpu_custom_call" | custom-call | tf_op jit(solution)/shard_map/pack/pallas_call | solution.py:147
  10.4 2.7 %pack.13 = bf16[18,96,128]{2,1,0:T(8,128)(2,1)} custom-call(s32[1]{0:T(128)} %bitcast.place, bf16[96,16,1024]{2,1,0:T(8,128)(2,1)} %refs_1_.7, bf16[96,16,1024]{2,1,0:T(8,128)(2,1)} %refs_1_.7, bf16[96,16,1024]{2,1,0:T(8,128)(2,1)} %refs_1_.7), custom_call_target="tpu_custom_call" | custom-call | tf_op jit(solution)/shard_map/pack/pallas_call | solution.py:147
  14.1 2.5 %pack.12 = bf16[17,96,128]{2,1,0:T(8,128)(2,1)} custom-call(s32[1]{0:T(128)} %bitcast.place, bf16[96,16,1024]{2,1,0:T(8,128)(2,1)} %refs_1_.7, bf16[96,16,1024]{2,1,0:T(8,128)(2,1)} %refs_1_.7), custom_call_target="tpu_custom_call" | custom-call | tf_op jit(solution)/shard_map/pack/pallas_call | solution.py:147
  16.6 2.5 %pack.10 = bf16[17,96,128]{2,1,0:T(8,128)(2,1)} custom-call(s32[1]{0:T(128)} %bitcast.place, bf16[96,16,1024]{2,1,0:T(8,128)(2,1)} %refs_1_.7, bf16[96,16,1024]{2,1,0:T(8,128)(2,1)} %refs_1_.7), custom_call_target="tpu_custom_call" | custom-call | tf_op jit(solution)/shard_map/pack/pallas_call | solution.py:147
  19.1 2.5 %pack.8.refs_0_ = bf16[17,96,128]{2,1,0:T(8,128)(2,1)} custom-call(s32[1]{0:T(128)} %bitcast.place, bf16[96,16,1024]{2,1,0:T(8,128)(2,1)} %refs_1_.7, bf16[96,16,1024]{2,1,0:T(8,128)(2,1)} %refs_1_.7), custom_call_target="tpu_custom_call" | custom-call | tf_op jit(solution)/shard_map/pack/pallas_call | solution.py:147
  21.6 2.5 %pack.14 = bf16[17,96,128]{2,1,0:T(8,128)(2,1)} custom-call(s32[1]{0:T(128)} %bitcast.place, bf16[96,16,1024]{2,1,0:T(8,128)(2,1)} %refs_1_.7, bf16[96,16,1024]{2,1,0:T(8,128)(2,1)} %refs_1_.7), custom_call_target="tpu_custom_call" | custom-call | tf_op jit(solution)/shard_map/pack/pallas_call | solution.py:147
  24.0 2.7 %pack.9.refs_0_ = bf16[18,96,128]{2,1,0:T(8,128)(2,1)} custom-call(s32[1]{0:T(128)} %bitcast.place, bf16[96,16,1024]{2,1,0:T(8,128)(2,1)} %refs_1_.7, bf16[96,16,1024]{2,1,0:T(8,128)(2,1)} %refs_1_.7, bf16[96,16,1024]{2,1,0:T(8,128)(2,1)} %refs_1_.7), custom_call_target="tpu_custom_call" | custom-call | tf_op jit(solution)/shard_map/pack/pallas_call | solution.py:147
  29.0 16.6 %collective-permute-done.2.refs_2_ = bf16[18,96,128]{2,1,0:T(8,128)(2,1)S(1)} collective-permute-done((bf16[18,96,128]{2,1,0:T(8,128)(2,1)}, bf16[18,96,128]{2,1,0:T(8,128)(2,1)S(1)}, u32[]{:S(2)}, u32[]{:S(2)}) %collective-permute-start.2) | collective-permute-done | bytes 442400 | tf_op jit(solution)/shard_map/ppermute | solution.py:386
  45.9 2.7 %collective-permute-start.7 = (bf16[7,384,128]{2,1,0:T(8,128)(2,1)S(1)}, bf16[7,384,128]{2,1,0:T(8,128)(2,1)S(1)}, u32[]{:S(2)}, u32[]{:S(2)}) collective-permute-start(bf16[7,384,128]{2,1,0:T(8,128)(2,1)S(1)} %pad_maximum_fusion.1), channel_id=1, source_target_pairs={{4,0},{8,4},{12,8},{16,12},{20,16},{24,20},{28,24},{0,28},{5,1},{9... | collective-permute-start | bytes 2064392 | tf_op jit(solution)/shard_map/ppermute | solution.py:412
  50.0 4.4 %collective-permute-start.5 = (bf16[17,96,128]{2,1,0:T(8,128)(2,1)S(1)}, bf16[17,96,128]{2,1,0:T(8,128)(2,1)S(1)}, u32[]{:S(2)}, u32[]{:S(2)}) collective-permute-start(bf16[17,96,128]{2,1,0:T(8,128)(2,1)S(1)} %copy-done.2), channel_id=1, source_target_pairs={{0,3},{1,0},{2,1},{3,2},{4,7},{5,4},{6,5},{7,6},{8,11},{9,8},{10,9... | collective-permute-start | bytes 1253384 | tf_op jit(solution)/shard_map/ppermute | solution.py:386
  55.1 7.4 %collective-permute-done.6.refs_4_ = bf16[7,384,128]{2,1,0:T(8,128)(2,1)S(1)} collective-permute-done((bf16[7,384,128]{2,1,0:T(8,128)(2,1)S(1)}, bf16[7,384,128]{2,1,0:T(8,128)(2,1)S(1)}, u32[]{:S(2)}, u32[]{:S(2)}) %collective-permute-start.6) | collective-permute-done | bytes 688160 | tf_op jit(solution)/shard_map/ppermute | solution.py:411
  62.5 16.6 %three_steps.2 = (bf16[16,96,128]{2,1,0:T(8,128)(2,1)S(1)}, bf16[16,96,128]{2,1,0:T(8,128)(2,1)S(1)}, bf16[16,96,128]{2,1,0:T(8,128)(2,1)S(1)}, bf16[16,96,128]{2,1,0:T(8,128)(2,1)S(1)}, f32[28,3,8,128]{3,2,1,0:T(8,128)S(1)}) custom-call(bf16[18,96,128]{2,1,0:T(8,128)(2,1)S(1)} %copy-done, bf16[18,96,128]{2,1,0:T(8,128)(2,1)S(1)} %collective-permute-done.refs_1_, ...), custom_call_target="tpu_custom_call" | custom-call | flops 6341787648 | bytes 8388608 | tf_op jit(solution)/shard_map/three_steps/pallas_call | solution.py:333
  79.2 9.2 %collective-permute-done.3.refs_2_ = bf16[17,96,128]{2,1,0:T(8,128)(2,1)S(1)} collective-permute-done((bf16[17,96,128]{2,1,0:T(8,128)(2,1)S(1)}, bf16[17,96,128]{2,1,0:T(8,128)(2,1)S(1)}, u32[]{:S(2)}, u32[]{:S(2)}) %collective-permute-start.3) | collective-permute-done | bytes 417824 | tf_op jit(solution)/shard_map/ppermute | solution.py:386
  89.6 2.7 %collective-permute-start.13 = (bf16[16,96,128]{2,1,0:T(8,128)(2,1)S(1)}, bf16[16,96,128]{2,1,0:T(8,128)(2,1)S(1)}, u32[]{:S(2)}, u32[]{:S(2)}) collective-permute-start(bf16[16,96,128]{2,1,0:T(8,128)(2,1)S(1)} %get-tuple-element.27), channel_id=1, source_target_pairs={{0,3},{1,0},{2,1},{3,2},{4,7},{5,4},{6,5},{7,6},{8,11},{9,8},{10,9... | collective-permute-start | bytes 1179656 | tf_op jit(solution)/shard_map/ppermute | solution.py:386
  92.9 9.9 %collective-permute-done.9.refs_5_ = bf16[7,384,128]{2,1,0:T(8,128)(2,1)S(1)} collective-permute-done((bf16[7,384,128]{2,1,0:T(8,128)(2,1)S(1)}, bf16[7,384,128]{2,1,0:T(8,128)(2,1)S(1)}, u32[]{:S(2)}, u32[]{:S(2)}) %collective-permute-start.9) | collective-permute-done | bytes 688160 | tf_op jit(solution)/shard_map/ppermute | solution.py:412
  102.8 3.7 %collective-permute-done.8.refs_4_ = bf16[7,384,128]{2,1,0:T(8,128)(2,1)S(1)} collective-permute-done((bf16[7,384,128]{2,1,0:T(8,128)(2,1)S(1)}, bf16[7,384,128]{2,1,0:T(8,128)(2,1)S(1)}, u32[]{:S(2)}, u32[]{:S(2)}) %collective-permute-start.8) | collective-permute-done | bytes 688160 | tf_op jit(solution)/shard_map/ppermute | solution.py:411
  106.5 16.6 %three_steps.3 = (bf16[16,96,128]{2,1,0:T(8,128)(2,1)S(1)}, bf16[16,96,128]{2,1,0:T(8,128)(2,1)S(1)}, bf16[16,96,128]{2,1,0:T(8,128)(2,1)S(1)}, bf16[16,96,128]{2,1,0:T(8,128)(2,1)S(1)}) custom-call(bf16[17,96,128]{2,1,0:T(8,128)(2,1)S(1)} %copy-done.1, bf16[17,96,128]{2,1,0:T(8,128)(2,1)S(1)} %collective-permute-done.1.refs_1_, ...), custom_call_target="tpu_custom_call" | custom-call | flops 6341787648 | bytes 8388608 | tf_op jit(solution)/shard_map/three_steps/pallas_call | solution.py:333
  123.0 2.7 %collective-permute-start.12 = (bf16[16,96,128]{2,1,0:T(8,128)(2,1)S(1)}, bf16[16,96,128]{2,1,0:T(8,128)(2,1)S(1)}, u32[]{:S(2)}, u32[]{:S(2)}) collective-permute-start(bf16[16,96,128]{2,1,0:T(8,128)(2,1)S(1)} %get-tuple-element.38), channel_id=1, source_target_pairs={{0,3},{1,0},{2,1},{3,2},{4,7},{5,4},{6,5},{7,6},{8,11},{9,8},{10,9... | collective-permute-start | bytes 1179656 | tf_op jit(solution)/shard_map/ppermute | solution.py:386
  126.4 2.7 %unpack.3.refs_2_ = bf16[96,16,1024]{2,1,0:T(8,128)(2,1)} custom-call(s32[1]{0:T(128)} %bitcast.place, bf16[16,96,128]{2,1,0:T(8,128)(2,1)S(1)} %get-tuple-element.26.refs_0_, bf16[16,96,128]{2,1,0:T(8,128)(2,1)S(1)} %collective-permute-done.13.refs_1_, bf16[16,96,128]{2,1,0:T(8,128)(2,1)S(1)} %collective-permute-done.14.refs_2_, ...), custom_call_target="tpu_custom_call" | custom-call | tf_op jit(solution)/shard_map/unpack/pallas_call | solution.py:187
  129.1 6.3 %collective-permute-done.12.refs_1_ = bf16[16,96,128]{2,1,0:T(8,128)(2,1)S(1)} collective-permute-done((bf16[16,96,128]{2,1,0:T(8,128)(2,1)S(1)}, bf16[16,96,128]{2,1,0:T(8,128)(2,1)S(1)}, u32[]{:S(2)}, u32[]{:S(2)}) %collective-permute-start.12) | collective-permute-done | bytes 393248 | tf_op jit(solution)/shard_map/ppermute | solution.py:386
  135.4 1.7 %unpack.4.refs_2_ = bf16[96,16,1024]{2,1,0:T(8,128)(2,1)} custom-call(s32[1]{0:T(128)} %bitcast.place, bf16[16,96,128]{2,1,0:T(8,128)(2,1)S(1)} %get-tuple-element.37.refs_0_, bf16[16,96,128]{2,1,0:T(8,128)(2,1)S(1)} %collective-permute-done.12.refs_1_, bf16[96,16,1024]{2,1,0:T(8,128)(2,1)} %unpack.3.refs_2_), custom_call_target="tpu_custom_call", output_to_operand_aliasing={{}: (3, {})} | custom-call | tf_op jit(solution)/shard_map/unpack/pallas_call | solution.py:187
  137.1 22.6 %collective-permute-done.10.refs_0_ = bf16[16,96,128]{2,1,0:T(8,128)(2,1)S(1)} collective-permute-done((bf16[16,96,128]{2,1,0:T(8,128)(2,1)S(1)}, bf16[16,96,128]{2,1,0:T(8,128)(2,1)S(1)}, u32[]{:S(2)}, u32[]{:S(2)}) %collective-permute-start.10) | collective-permute-done | bytes 393248 | tf_op jit(solution)/shard_map/ppermute | solution.py:386
  (87 shorter events, 9.6 us)
Async XLA Ops:
  2.6 26.3 %collective-permute-start.4 = (bf16[18,96,128]{2,1,0:T(8,128)(2,1)}, bf16[18,96,128]{2,1,0:T(8,128)(2,1)S(1)}, u32[]{:S(2)}, u32[]{:S(2)}) collective-permute-start(bf16[18,96,128]{2,1,0:T(8,128)(2,1)} %pack.15), channel_id=1, source_target_pairs={{0,3},{1,0},{2,1},{3,2},{4,7},{5,4},{6,5},{7,6},{8,11},{9,8},{10,9... | collective-permute-start | bytes 1327112 | tf_op jit(solution)/shard_map/ppermute | solution.py:386
  10.4 3.7 %copy-start.6 = (s32[384,6]{0,1:T(8,128)S(1)}, s32[384,6]{0,1:T(8,128)}, u32[]{:S(2)}) copy-start(s32[384,6]{0,1:T(8,128)} %param.9) | copy-start | bytes 27652
  10.4 18.6 %collective-permute-start = (bf16[18,96,128]{2,1,0:T(8,128)(2,1)}, bf16[18,96,128]{2,1,0:T(8,128)(2,1)S(1)}, u32[]{:S(2)}, u32[]{:S(2)}) collective-permute-start(bf16[18,96,128]{2,1,0:T(8,128)(2,1)} %pack.11), channel_id=1, source_target_pairs={{0,1},{1,2},{2,3},{3,0},{4,5},{5,6},{6,7},{7,4},{8,9},{9,10},{10,1... | collective-permute-start | bytes 1327112 | tf_op jit(solution)/shard_map/ppermute | solution.py:386
  13.1 32.6 %collective-permute-start.2 = (bf16[18,96,128]{2,1,0:T(8,128)(2,1)}, bf16[18,96,128]{2,1,0:T(8,128)(2,1)S(1)}, u32[]{:S(2)}, u32[]{:S(2)}) collective-permute-start(bf16[18,96,128]{2,1,0:T(8,128)(2,1)} %pack.13), channel_id=1, source_target_pairs={{0,2},{1,3},{2,0},{3,1},{4,6},{5,7},{6,4},{7,5},{8,10},{9,11},{10,... | collective-permute-start | bytes 1327112 | tf_op jit(solution)/shard_map/ppermute | solution.py:386
  24.0 2.9 %copy-start.9 = (f32[2,384]{1,0:T(2,128)S(1)}, f32[2,384]{1,0:T(2,128)}, u32[]{:S(2)}) copy-start(f32[2,384]{1,0:T(2,128)} %param.11) | copy-start | bytes 9220
  24.0 3.1 %copy-start.5 = (bf16[384,384]{1,0:T(8,128)(2,1)S(1)}, bf16[384,384]{1,0:T(8,128)(2,1)}, u32[]{:S(2)}) copy-start(bf16[384,384]{1,0:T(8,128)(2,1)} %param.7) | copy-start | bytes 884740
  24.0 3.7 %copy-start.7 = (s32[384,6]{0,1:T(8,128)S(1)}, s32[384,6]{0,1:T(8,128)}, u32[]{:S(2)}) copy-start(s32[384,6]{0,1:T(8,128)} %param.8) | copy-start | bytes 27652
  45.8 16.7 %collective-permute-start.6 = (bf16[7,384,128]{2,1,0:T(8,128)(2,1)S(1)}, bf16[7,384,128]{2,1,0:T(8,128)(2,1)S(1)}, u32[]{:S(2)}, u32[]{:S(2)}) collective-permute-start(bf16[7,384,128]{2,1,0:T(8,128)(2,1)S(1)} %pad_maximum_fusion), channel_id=1, source_target_pairs={{0,4},{4,8},{8,12},{12,16},{16,20},{20,24},{24,28},{28,0},{1,5},{5... | collective-permute-start | bytes 2064392 | tf_op jit(solution)/shard_map/ppermute | solution.py:411
  45.9 16.7 %collective-permute-start.7 = (bf16[7,384,128]{2,1,0:T(8,128)(2,1)S(1)}, bf16[7,384,128]{2,1,0:T(8,128)(2,1)S(1)}, u32[]{:S(2)}, u32[]{:S(2)}) collective-permute-start(bf16[7,384,128]{2,1,0:T(8,128)(2,1)S(1)} %pad_maximum_fusion.1), channel_id=1, source_target_pairs={{4,0},{8,4},{12,8},{16,12},{20,16},{24,20},{28,24},{0,28},{5,1},{9... | collective-permute-start | bytes 2064392 | tf_op jit(solution)/shard_map/ppermute | solution.py:412
  49.0 5.4 %copy-start.4 = (bf16[17,96,128]{2,1,0:T(8,128)(2,1)S(1)}, bf16[17,96,128]{2,1,0:T(8,128)(2,1)}, u32[]{:S(2)}) copy-start(bf16[17,96,128]{2,1,0:T(8,128)(2,1)} %pack.10) | copy-start | bytes 1253380
  49.0 5.4 %copy-start.3 = (bf16[17,96,128]{2,1,0:T(8,128)(2,1)S(1)}, bf16[17,96,128]{2,1,0:T(8,128)(2,1)}, u32[]{:S(2)}) copy-start(bf16[17,96,128]{2,1,0:T(8,128)(2,1)} %pack.12) | copy-start | bytes 1253380
  50.0 38.5 %collective-permute-start.5 = (bf16[17,96,128]{2,1,0:T(8,128)(2,1)S(1)}, bf16[17,96,128]{2,1,0:T(8,128)(2,1)S(1)}, u32[]{:S(2)}, u32[]{:S(2)}) collective-permute-start(bf16[17,96,128]{2,1,0:T(8,128)(2,1)S(1)} %copy-done.2), channel_id=1, source_target_pairs={{0,3},{1,0},{2,1},{3,2},{4,7},{5,4},{6,5},{7,6},{8,11},{9,8},{10,9... | collective-permute-start | bytes 1253384 | tf_op jit(solution)/shard_map/ppermute | solution.py:386
  54.4 24.8 %collective-permute-start.1 = (bf16[17,96,128]{2,1,0:T(8,128)(2,1)S(1)}, bf16[17,96,128]{2,1,0:T(8,128)(2,1)S(1)}, u32[]{:S(2)}, u32[]{:S(2)}) collective-permute-start(bf16[17,96,128]{2,1,0:T(8,128)(2,1)S(1)} %copy-done.4), channel_id=1, source_target_pairs={{0,1},{1,2},{2,3},{3,0},{4,5},{5,6},{6,7},{7,4},{8,9},{9,10},{10,1... | collective-permute-start | bytes 1253384 | tf_op jit(solution)/shard_map/ppermute | solution.py:386
  54.4 34.1 %collective-permute-start.3 = (bf16[17,96,128]{2,1,0:T(8,128)(2,1)S(1)}, bf16[17,96,128]{2,1,0:T(8,128)(2,1)S(1)}, u32[]{:S(2)}, u32[]{:S(2)}) collective-permute-start(bf16[17,96,128]{2,1,0:T(8,128)(2,1)S(1)} %copy-done.3), channel_id=1, source_target_pairs={{0,2},{1,3},{2,0},{3,1},{4,6},{5,7},{6,4},{7,5},{8,10},{9,11},{10,... | collective-permute-start | bytes 1253384 | tf_op jit(solution)/shard_map/ppermute | solution.py:386
  79.2 9.4 %slice-start.2 = ((bf16[17,96,128]{2,1,0:T(8,128)(2,1)}), bf16[7,96,128]{2,1,0:T(8,128)(2,1)S(1)}, s32[]{:S(2)}) async-start(bf16[17,96,128]{2,1,0:T(8,128)(2,1)} %pack.8.refs_0_), calls=%async_computation.2 | async-start | bytes 344064 | tf_op jit(solution)/shard_map/slice | solution.py:404
  88.6 17.8 %copy-start.1 = (bf16[17,96,128]{2,1,0:T(8,128)(2,1)S(1)}, bf16[17,96,128]{2,1,0:T(8,128)(2,1)}, u32[]{:S(2)}) copy-start(bf16[17,96,128]{2,1,0:T(8,128)(2,1)} %pack.8.refs_0_) | copy-start | bytes 1253380
  88.7 14.1 %collective-permute-start.9 = (bf16[7,384,128]{2,1,0:T(8,128)(2,1)S(1)}, bf16[7,384,128]{2,1,0:T(8,128)(2,1)S(1)}, u32[]{:S(2)}, u32[]{:S(2)}) collective-permute-start(bf16[7,384,128]{2,1,0:T(8,128)(2,1)S(1)} %pad_maximum_fusion.2), channel_id=1, source_target_pairs={{4,0},{8,4},{12,8},{16,12},{20,16},{24,20},{28,24},{0,28},{5,1},{9... | collective-permute-start | bytes 2064392 | tf_op jit(solution)/shard_map/ppermute | solution.py:412
  89.5 17.0 %collective-permute-start.8 = (bf16[7,384,128]{2,1,0:T(8,128)(2,1)S(1)}, bf16[7,384,128]{2,1,0:T(8,128)(2,1)S(1)}, u32[]{:S(2)}, u32[]{:S(2)}) collective-permute-start(bf16[7,384,128]{2,1,0:T(8,128)(2,1)S(1)} %maximum_maximum_fusion), channel_id=1, source_target_pairs={{0,4},{4,8},{8,12},{12,16},{16,20},{20,24},{24,28},{28,0},{1,5},{5... | collective-permute-start | bytes 2064392 | tf_op jit(solution)/shard_map/ppermute | solution.py:411
  89.6 36.2 %collective-permute-start.13 = (bf16[16,96,128]{2,1,0:T(8,128)(2,1)S(1)}, bf16[16,96,128]{2,1,0:T(8,128)(2,1)S(1)}, u32[]{:S(2)}, u32[]{:S(2)}) collective-permute-start(bf16[16,96,128]{2,1,0:T(8,128)(2,1)S(1)} %get-tuple-element.27), channel_id=1, source_target_pairs={{0,3},{1,0},{2,1},{3,2},{4,7},{5,4},{6,5},{7,6},{8,11},{9,8},{10,9... | collective-permute-start | bytes 1179656 | tf_op jit(solution)/shard_map/ppermute | solution.py:386
  92.3 34.1 %collective-permute-start.14 = (bf16[16,96,128]{2,1,0:T(8,128)(2,1)S(1)}, bf16[16,96,128]{2,1,0:T(8,128)(2,1)S(1)}, u32[]{:S(2)}, u32[]{:S(2)}) collective-permute-start(bf16[16,96,128]{2,1,0:T(8,128)(2,1)S(1)} %get-tuple-element.28), channel_id=1, source_target_pairs={{0,2},{1,3},{2,0},{3,1},{4,6},{5,7},{6,4},{7,5},{8,10},{9,11},{10,... | collective-permute-start | bytes 1179656 | tf_op jit(solution)/shard_map/ppermute | solution.py:386
  92.3 34.1 %collective-permute-start.15 = (bf16[16,96,128]{2,1,0:T(8,128)(2,1)S(1)}, bf16[16,96,128]{2,1,0:T(8,128)(2,1)S(1)}, u32[]{:S(2)}, u32[]{:S(2)}) collective-permute-start(bf16[16,96,128]{2,1,0:T(8,128)(2,1)S(1)} %get-tuple-element.29), channel_id=1, source_target_pairs={{0,1},{1,2},{2,3},{3,0},{4,5},{5,6},{6,7},{7,4},{8,9},{9,10},{10,1... | collective-permute-start | bytes 1179656 | tf_op jit(solution)/shard_map/ppermute | solution.py:386
  123.0 12.3 %collective-permute-start.12 = (bf16[16,96,128]{2,1,0:T(8,128)(2,1)S(1)}, bf16[16,96,128]{2,1,0:T(8,128)(2,1)S(1)}, u32[]{:S(2)}, u32[]{:S(2)}) collective-permute-start(bf16[16,96,128]{2,1,0:T(8,128)(2,1)S(1)} %get-tuple-element.38), channel_id=1, source_target_pairs={{0,3},{1,0},{2,1},{3,2},{4,7},{5,4},{6,5},{7,6},{8,11},{9,8},{10,9... | collective-permute-start | bytes 1179656 | tf_op jit(solution)/shard_map/ppermute | solution.py:386
  125.7 34.0 %collective-permute-start.10 = (bf16[16,96,128]{2,1,0:T(8,128)(2,1)S(1)}, bf16[16,96,128]{2,1,0:T(8,128)(2,1)S(1)}, u32[]{:S(2)}, u32[]{:S(2)}) collective-permute-start(bf16[16,96,128]{2,1,0:T(8,128)(2,1)S(1)} %get-tuple-element.35), channel_id=1, source_target_pairs={{0,2},{1,3},{2,0},{3,1},{4,6},{5,7},{6,4},{7,5},{8,10},{9,11},{10,... | collective-permute-start | bytes 1179656 | tf_op jit(solution)/shard_map/ppermute | solution.py:386
  125.8 34.0 %collective-permute-start.11 = (bf16[16,96,128]{2,1,0:T(8,128)(2,1)S(1)}, bf16[16,96,128]{2,1,0:T(8,128)(2,1)S(1)}, u32[]{:S(2)}, u32[]{:S(2)}) collective-permute-start(bf16[16,96,128]{2,1,0:T(8,128)(2,1)S(1)} %get-tuple-element.36), channel_id=1, source_target_pairs={{0,1},{1,2},{2,3},{3,0},{4,5},{5,6},{6,7},{7,4},{8,9},{9,10},{10,1... | collective-permute-start | bytes 1179656 | tf_op jit(solution)/shard_map/ppermute | solution.py:386
  (5 other events, 6.6 us)

commit v4 on v3

--- a/solution.py
+++ b/solution.py
@@ -419,7 +419,7 @@
         result = results[part]
         returned = [result[0]] + [ahead(result[shift], devices - shift) for shift in range(1, devices)]
         middle = devices // 2 if part + 1 == parts else devices
-        for shifts in (range(middle), range(middle, devices)):
+        for shifts in (range(middle), *[(shift,) for shift in range(middle, devices)]):
             if len(shifts):
                 evolved = unpack(returned, shifts, place, part, parts, density.shape, evolved)
     return evolved

time: 162 us -> 163 us (level)
    pallas_call x3 -> x4, Pallas kernels: 6.12 us -> 6.88 us  [unpack(): pl.pallas_call(functools.partial(unpack_kernel, devices, shifts, part, pa...]
  transfers between devices with their start and end apart: 16 -> 16, of which waited for: 8 -> 8; matrix products, arithmetic and copies ran while one was open for 2% -> 2% of each run, Pallas kernels for 34% -> 35%
where the time goes in v4:
time: 163 us; the launch traced here: 162 us
  waiting for transfers between devices  75.8 us (47%)
  Pallas kernels  60.7 us (37%)
  starting transfers between devices  20.7 us (13%)
  local copies, waits for them, and re-layouts  2.83 us (2%)
  other arithmetic  1.74 us (1%)
    ppermute x12, waiting for transfers between devices, ahead(): lax.ppermute(value, 'ao', [(i, (i + shift) % devices) for i in range(devi...  54.8 us
    pallas_call x2, Pallas kernels, three_steps(): pl.pallas_call(functools.partial(steps_kernel, devices, edge is not None,...  33.2 us
    pallas_call x8, Pallas kernels, pack(): pl.pallas_call(pack_kernel, grid_spec=pltpu.PrefetchScalarGridSpec(num_sc...  20.7 us
    ppermute x12, starting transfers between devices, ahead(): lax.ppermute(value, 'ao', [(i, (i + shift) % devices) for i in range(devi...  17.8 us
    ppermute x2, waiting for transfers between devices, blocked(): above = lax.ppermute(upper, 'gx', up)  11.1 us
    ppermute x2, waiting for transfers between devices, blocked(): below = lax.ppermute(joint(0, REACH + 1), 'gx', down)  9.98 us
    pallas_call x4, Pallas kernels, unpack(): pl.pallas_call(functools.partial(unpack_kernel, devices, shifts, part, pa...  6.88 us
  transfers between devices with their start and end apart: 16, of which 8 were waited for; matrix products, arithmetic and copies ran while one was open for 2% of the time, Pallas kernels for 35%

profile of v4, /device:TPU:0, one launch (start us, length us, event | category | flops | bytes accessed | tf_op | source)
XLA Modules:
  0.0 162.4 jit_solution(10097331042370533426)
XLA Ops:
  0.0 2.6 %pack.15 = bf16[18,96,128]{2,1,0:T(8,128)(2,1)} custom-call(s32[1]{0:T(128)} %bitcast.place, bf16[96,16,1024]{2,1,0:T(8,128)(2,1)} %refs_1_.7, bf16[96,16,1024]{2,1,0:T(8,128)(2,1)} %refs_1_.7, bf16[96,16,1024]{2,1,0:T(8,128)(2,1)} %refs_1_.7), custom_call_target="tpu_custom_call" | custom-call | tf_op jit(solution)/shard_map/pack/pallas_call | solution.py:147
  2.6 5.0 %collective-permute-start.4 = (bf16[18,96,128]{2,1,0:T(8,128)(2,1)}, bf16[18,96,128]{2,1,0:T(8,128)(2,1)S(1)}, u32[]{:S(2)}, u32[]{:S(2)}) collective-permute-start(bf16[18,96,128]{2,1,0:T(8,128)(2,1)} %pack.15), channel_id=1, source_target_pairs={{0,3},{1,0},{2,1},{3,2},{4,7},{5,4},{6,5},{7,6},{8,11},{9,8},{10,9... | collective-permute-start | bytes 1327112 | tf_op jit(solution)/shard_map/ppermute | solution.py:386
  7.7 2.7 %pack.11 = bf16[18,96,128]{2,1,0:T(8,128)(2,1)} custom-call(s32[1]{0:T(128)} %bitcast.place, bf16[96,16,1024]{2,1,0:T(8,128)(2,1)} %refs_1_.7, bf16[96,16,1024]{2,1,0:T(8,128)(2,1)} %refs_1_.7, bf16[96,16,1024]{2,1,0:T(8,128)(2,1)} %refs_1_.7), custom_call_target="tpu_custom_call" | custom-call | tf_op jit(solution)/shard_map/pack/pallas_call | solution.py:147
  10.4 2.7 %pack.13 = bf16[18,96,128]{2,1,0:T(8,128)(2,1)} custom-call(s32[1]{0:T(128)} %bitcast.place, bf16[96,16,1024]{2,1,0:T(8,128)(2,1)} %refs_1_.7, bf16[96,16,1024]{2,1,0:T(8,128)(2,1)} %refs_1_.7, bf16[96,16,1024]{2,1,0:T(8,128)(2,1)} %refs_1_.7), custom_call_target="tpu_custom_call" | custom-call | tf_op jit(solution)/shard_map/pack/pallas_call | solution.py:147
  14.1 2.5 %pack.12 = bf16[17,96,128]{2,1,0:T(8,128)(2,1)} custom-call(s32[1]{0:T(128)} %bitcast.place, bf16[96,16,1024]{2,1,0:T(8,128)(2,1)} %refs_1_.7, bf16[96,16,1024]{2,1,0:T(8,128)(2,1)} %refs_1_.7), custom_call_target="tpu_custom_call" | custom-call | tf_op jit(solution)/shard_map/pack/pallas_call | solution.py:147
  16.6 2.5 %pack.10 = bf16[17,96,128]{2,1,0:T(8,128)(2,1)} custom-call(s32[1]{0:T(128)} %bitcast.place, bf16[96,16,1024]{2,1,0:T(8,128)(2,1)} %refs_1_.7, bf16[96,16,1024]{2,1,0:T(8,128)(2,1)} %refs_1_.7), custom_call_target="tpu_custom_call" | custom-call | tf_op jit(solution)/shard_map/pack/pallas_call | solution.py:147
  19.1 2.5 %pack.8.refs_0_ = bf16[17,96,128]{2,1,0:T(8,128)(2,1)} custom-call(s32[1]{0:T(128)} %bitcast.place, bf16[96,16,1024]{2,1,0:T(8,128)(2,1)} %refs_1_.7, bf16[96,16,1024]{2,1,0:T(8,128)(2,1)} %refs_1_.7), custom_call_target="tpu_custom_call" | custom-call | tf_op jit(solution)/shard_map/pack/pallas_call | solution.py:147
  21.6 2.5 %pack.14 = bf16[17,96,128]{2,1,0:T(8,128)(2,1)} custom-call(s32[1]{0:T(128)} %bitcast.place, bf16[96,16,1024]{2,1,0:T(8,128)(2,1)} %refs_1_.7, bf16[96,16,1024]{2,1,0:T(8,128)(2,1)} %refs_1_.7), custom_call_target="tpu_custom_call" | custom-call | tf_op jit(solution)/shard_map/pack/pallas_call | solution.py:147
  24.0 2.7 %pack.9.refs_0_ = bf16[18,96,128]{2,1,0:T(8,128)(2,1)} custom-call(s32[1]{0:T(128)} %bitcast.place, bf16[96,16,1024]{2,1,0:T(8,128)(2,1)} %refs_1_.7, bf16[96,16,1024]{2,1,0:T(8,128)(2,1)} %refs_1_.7, bf16[96,16,1024]{2,1,0:T(8,128)(2,1)} %refs_1_.7), custom_call_target="tpu_custom_call" | custom-call | tf_op jit(solution)/shard_map/pack/pallas_call | solution.py:147
  29.0 16.6 %collective-permute-done.2.refs_2_ = bf16[18,96,128]{2,1,0:T(8,128)(2,1)S(1)} collective-permute-done((bf16[18,96,128]{2,1,0:T(8,128)(2,1)}, bf16[18,96,128]{2,1,0:T(8,128)(2,1)S(1)}, u32[]{:S(2)}, u32[]{:S(2)}) %collective-permute-start.2) | collective-permute-done | bytes 442400 | tf_op jit(solution)/shard_map/ppermute | solution.py:386
  45.9 2.7 %collective-permute-start.7 = (bf16[7,384,128]{2,1,0:T(8,128)(2,1)S(1)}, bf16[7,384,128]{2,1,0:T(8,128)(2,1)S(1)}, u32[]{:S(2)}, u32[]{:S(2)}) collective-permute-start(bf16[7,384,128]{2,1,0:T(8,128)(2,1)S(1)} %pad_maximum_fusion.1), channel_id=1, source_target_pairs={{4,0},{8,4},{12,8},{16,12},{20,16},{24,20},{28,24},{0,28},{5,1},{9... | collective-permute-start | bytes 2064392 | tf_op jit(solution)/shard_map/ppermute | solution.py:412
  50.0 4.4 %collective-permute-start.5 = (bf16[17,96,128]{2,1,0:T(8,128)(2,1)S(1)}, bf16[17,96,128]{2,1,0:T(8,128)(2,1)S(1)}, u32[]{:S(2)}, u32[]{:S(2)}) collective-permute-start(bf16[17,96,128]{2,1,0:T(8,128)(2,1)S(1)} %copy-done.2), channel_id=1, source_target_pairs={{0,3},{1,0},{2,1},{3,2},{4,7},{5,4},{6,5},{7,6},{8,11},{9,8},{10,9... | collective-permute-start | bytes 1253384 | tf_op jit(solution)/shard_map/ppermute | solution.py:386
  55.1 7.4 %collective-permute-done.6.refs_4_ = bf16[7,384,128]{2,1,0:T(8,128)(2,1)S(1)} collective-permute-done((bf16[7,384,128]{2,1,0:T(8,128)(2,1)S(1)}, bf16[7,384,128]{2,1,0:T(8,128)(2,1)S(1)}, u32[]{:S(2)}, u32[]{:S(2)}) %collective-permute-start.6) | collective-permute-done | bytes 688160 | tf_op jit(solution)/shard_map/ppermute | solution.py:411
  62.5 16.6 %three_steps.2 = (bf16[16,96,128]{2,1,0:T(8,128)(2,1)S(1)}, bf16[16,96,128]{2,1,0:T(8,128)(2,1)S(1)}, bf16[16,96,128]{2,1,0:T(8,128)(2,1)S(1)}, bf16[16,96,128]{2,1,0:T(8,128)(2,1)S(1)}, f32[28,3,8,128]{3,2,1,0:T(8,128)S(1)}) custom-call(bf16[18,96,128]{2,1,0:T(8,128)(2,1)S(1)} %copy-done, bf16[18,96,128]{2,1,0:T(8,128)(2,1)S(1)} %collective-permute-done.refs_1_, ...), custom_call_target="tpu_custom_call" | custom-call | flops 6341787648 | bytes 8388608 | tf_op jit(solution)/shard_map/three_steps/pallas_call | solution.py:333
  79.2 9.2 %collective-permute-done.3.refs_2_ = bf16[17,96,128]{2,1,0:T(8,128)(2,1)S(1)} collective-permute-done((bf16[17,96,128]{2,1,0:T(8,128)(2,1)S(1)}, bf16[17,96,128]{2,1,0:T(8,128)(2,1)S(1)}, u32[]{:S(2)}, u32[]{:S(2)}) %collective-permute-start.3) | collective-permute-done | bytes 417824 | tf_op jit(solution)/shard_map/ppermute | solution.py:386
  89.6 2.7 %collective-permute-start.13 = (bf16[16,96,128]{2,1,0:T(8,128)(2,1)S(1)}, bf16[16,96,128]{2,1,0:T(8,128)(2,1)S(1)}, u32[]{:S(2)}, u32[]{:S(2)}) collective-permute-start(bf16[16,96,128]{2,1,0:T(8,128)(2,1)S(1)} %get-tuple-element.27), channel_id=1, source_target_pairs={{0,3},{1,0},{2,1},{3,2},{4,7},{5,4},{6,5},{7,6},{8,11},{9,8},{10,9... | collective-permute-start | bytes 1179656 | tf_op jit(solution)/shard_map/ppermute | solution.py:386
  92.9 9.9 %collective-permute-done.9.refs_5_ = bf16[7,384,128]{2,1,0:T(8,128)(2,1)S(1)} collective-permute-done((bf16[7,384,128]{2,1,0:T(8,128)(2,1)S(1)}, bf16[7,384,128]{2,1,0:T(8,128)(2,1)S(1)}, u32[]{:S(2)}, u32[]{:S(2)}) %collective-permute-start.9) | collective-permute-done | bytes 688160 | tf_op jit(solution)/shard_map/ppermute | solution.py:412
  102.8 3.7 %collective-permute-done.8.refs_4_ = bf16[7,384,128]{2,1,0:T(8,128)(2,1)S(1)} collective-permute-done((bf16[7,384,128]{2,1,0:T(8,128)(2,1)S(1)}, bf16[7,384,128]{2,1,0:T(8,128)(2,1)S(1)}, u32[]{:S(2)}, u32[]{:S(2)}) %collective-permute-start.8) | collective-permute-done | bytes 688160 | tf_op jit(solution)/shard_map/ppermute | solution.py:411
  106.5 16.6 %three_steps.3 = (bf16[16,96,128]{2,1,0:T(8,128)(2,1)S(1)}, bf16[16,96,128]{2,1,0:T(8,128)(2,1)S(1)}, bf16[16,96,128]{2,1,0:T(8,128)(2,1)S(1)}, bf16[16,96,128]{2,1,0:T(8,128)(2,1)S(1)}) custom-call(bf16[17,96,128]{2,1,0:T(8,128)(2,1)S(1)} %copy-done.1, bf16[17,96,128]{2,1,0:T(8,128)(2,1)S(1)} %collective-permute-done.1.refs_1_, ...), custom_call_target="tpu_custom_call" | custom-call | flops 6341787648 | bytes 8388608 | tf_op jit(solution)/shard_map/three_steps/pallas_call | solution.py:333
  123.0 2.7 %collective-permute-start.12 = (bf16[16,96,128]{2,1,0:T(8,128)(2,1)S(1)}, bf16[16,96,128]{2,1,0:T(8,128)(2,1)S(1)}, u32[]{:S(2)}, u32[]{:S(2)}) collective-permute-start(bf16[16,96,128]{2,1,0:T(8,128)(2,1)S(1)} %get-tuple-element.38), channel_id=1, source_target_pairs={{0,3},{1,0},{2,1},{3,2},{4,7},{5,4},{6,5},{7,6},{8,11},{9,8},{10,9... | collective-permute-start | bytes 1179656 | tf_op jit(solution)/shard_map/ppermute | solution.py:386
  126.4 2.7 %unpack.4.refs_2_ = bf16[96,16,1024]{2,1,0:T(8,128)(2,1)} custom-call(s32[1]{0:T(128)} %bitcast.place, bf16[16,96,128]{2,1,0:T(8,128)(2,1)S(1)} %get-tuple-element.26.refs_0_, bf16[16,96,128]{2,1,0:T(8,128)(2,1)S(1)} %collective-permute-done.13.refs_1_, bf16[16,96,128]{2,1,0:T(8,128)(2,1)S(1)} %collective-permute-done.14.refs_2_, ...), custom_call_target="tpu_custom_call" | custom-call | tf_op jit(solution)/shard_map/unpack/pallas_call | solution.py:187
  129.1 6.3 %collective-permute-done.12.refs_1_ = bf16[16,96,128]{2,1,0:T(8,128)(2,1)S(1)} collective-permute-done((bf16[16,96,128]{2,1,0:T(8,128)(2,1)S(1)}, bf16[16,96,128]{2,1,0:T(8,128)(2,1)S(1)}, u32[]{:S(2)}, u32[]{:S(2)}) %collective-permute-start.12) | collective-permute-done | bytes 393248 | tf_op jit(solution)/shard_map/ppermute | solution.py:386
  135.4 1.7 %unpack.5.refs_1_ = bf16[96,16,1024]{2,1,0:T(8,128)(2,1)} custom-call(s32[1]{0:T(128)} %bitcast.place, bf16[16,96,128]{2,1,0:T(8,128)(2,1)S(1)} %get-tuple-element.37.refs_0_, bf16[16,96,128]{2,1,0:T(8,128)(2,1)S(1)} %collective-permute-done.12.refs_1_, bf16[96,16,1024]{2,1,0:T(8,128)(2,1)} %unpack.4.refs_2_), custom_call_target="tpu_custom_call", output_to_operand_aliasing={{}: (3, {})} | custom-call | tf_op jit(solution)/shard_map/unpack/pallas_call | solution.py:187
  137.1 22.6 %collective-permute-done.11.refs_0_ = bf16[16,96,128]{2,1,0:T(8,128)(2,1)S(1)} collective-permute-done((bf16[16,96,128]{2,1,0:T(8,128)(2,1)S(1)}, bf16[16,96,128]{2,1,0:T(8,128)(2,1)S(1)}, u32[]{:S(2)}, u32[]{:S(2)}) %collective-permute-start.11) | collective-permute-done | bytes 393248 | tf_op jit(solution)/shard_map/ppermute | solution.py:386
  (88 shorter events, 10.3 us)
Async XLA Ops:
  2.6 26.3 %collective-permute-start.4 = (bf16[18,96,128]{2,1,0:T(8,128)(2,1)}, bf16[18,96,128]{2,1,0:T(8,128)(2,1)S(1)}, u32[]{:S(2)}, u32[]{:S(2)}) collective-permute-start(bf16[18,96,128]{2,1,0:T(8,128)(2,1)} %pack.15), channel_id=1, source_target_pairs={{0,3},{1,0},{2,1},{3,2},{4,7},{5,4},{6,5},{7,6},{8,11},{9,8},{10,9... | collective-permute-start | bytes 1327112 | tf_op jit(solution)/shard_map/ppermute | solution.py:386
  10.4 3.7 %copy-start.6 = (s32[384,6]{0,1:T(8,128)S(1)}, s32[384,6]{0,1:T(8,128)}, u32[]{:S(2)}) copy-start(s32[384,6]{0,1:T(8,128)} %param.9) | copy-start | bytes 27652
  10.4 18.6 %collective-permute-start = (bf16[18,96,128]{2,1,0:T(8,128)(2,1)}, bf16[18,96,128]{2,1,0:T(8,128)(2,1)S(1)}, u32[]{:S(2)}, u32[]{:S(2)}) collective-permute-start(bf16[18,96,128]{2,1,0:T(8,128)(2,1)} %pack.11), channel_id=1, source_target_pairs={{0,1},{1,2},{2,3},{3,0},{4,5},{5,6},{6,7},{7,4},{8,9},{9,10},{10,1... | collective-permute-start | bytes 1327112 | tf_op jit(solution)/shard_map/ppermute | solution.py:386
  13.1 32.6 %collective-permute-start.2 = (bf16[18,96,128]{2,1,0:T(8,128)(2,1)}, bf16[18,96,128]{2,1,0:T(8,128)(2,1)S(1)}, u32[]{:S(2)}, u32[]{:S(2)}) collective-permute-start(bf16[18,96,128]{2,1,0:T(8,128)(2,1)} %pack.13), channel_id=1, source_target_pairs={{0,2},{1,3},{2,0},{3,1},{4,6},{5,7},{6,4},{7,5},{8,10},{9,11},{10,... | collective-permute-start | bytes 1327112 | tf_op jit(solution)/shard_map/ppermute | solution.py:386
  24.0 2.9 %copy-start.9 = (f32[2,384]{1,0:T(2,128)S(1)}, f32[2,384]{1,0:T(2,128)}, u32[]{:S(2)}) copy-start(f32[2,384]{1,0:T(2,128)} %param.11) | copy-start | bytes 9220
  24.0 3.1 %copy-start.5 = (bf16[384,384]{1,0:T(8,128)(2,1)S(1)}, bf16[384,384]{1,0:T(8,128)(2,1)}, u32[]{:S(2)}) copy-start(bf16[384,384]{1,0:T(8,128)(2,1)} %param.7) | copy-start | bytes 884740
  24.0 3.7 %copy-start.7 = (s32[384,6]{0,1:T(8,128)S(1)}, s32[384,6]{0,1:T(8,128)}, u32[]{:S(2)}) copy-start(s32[384,6]{0,1:T(8,128)} %param.8) | copy-start | bytes 27652
  45.8 16.7 %collective-permute-start.6 = (bf16[7,384,128]{2,1,0:T(8,128)(2,1)S(1)}, bf16[7,384,128]{2,1,0:T(8,128)(2,1)S(1)}, u32[]{:S(2)}, u32[]{:S(2)}) collective-permute-start(bf16[7,384,128]{2,1,0:T(8,128)(2,1)S(1)} %pad_maximum_fusion), channel_id=1, source_target_pairs={{0,4},{4,8},{8,12},{12,16},{16,20},{20,24},{24,28},{28,0},{1,5},{5... | collective-permute-start | bytes 2064392 | tf_op jit(solution)/shard_map/ppermute | solution.py:411
  45.9 16.7 %collective-permute-start.7 = (bf16[7,384,128]{2,1,0:T(8,128)(2,1)S(1)}, bf16[7,384,128]{2,1,0:T(8,128)(2,1)S(1)}, u32[]{:S(2)}, u32[]{:S(2)}) collective-permute-start(bf16[7,384,128]{2,1,0:T(8,128)(2,1)S(1)} %pad_maximum_fusion.1), channel_id=1, source_target_pairs={{4,0},{8,4},{12,8},{16,12},{20,16},{24,20},{28,24},{0,28},{5,1},{9... | collective-permute-start | bytes 2064392 | tf_op jit(solution)/shard_map/ppermute | solution.py:412
  49.0 5.4 %copy-start.4 = (bf16[17,96,128]{2,1,0:T(8,128)(2,1)S(1)}, bf16[17,96,128]{2,1,0:T(8,128)(2,1)}, u32[]{:S(2)}) copy-start(bf16[17,96,128]{2,1,0:T(8,128)(2,1)} %pack.10) | copy-start | bytes 1253380
  49.0 5.4 %copy-start.3 = (bf16[17,96,128]{2,1,0:T(8,128)(2,1)S(1)}, bf16[17,96,128]{2,1,0:T(8,128)(2,1)}, u32[]{:S(2)}) copy-start(bf16[17,96,128]{2,1,0:T(8,128)(2,1)} %pack.12) | copy-start | bytes 1253380
  50.0 38.5 %collective-permute-start.5 = (bf16[17,96,128]{2,1,0:T(8,128)(2,1)S(1)}, bf16[17,96,128]{2,1,0:T(8,128)(2,1)S(1)}, u32[]{:S(2)}, u32[]{:S(2)}) collective-permute-start(bf16[17,96,128]{2,1,0:T(8,128)(2,1)S(1)} %copy-done.2), channel_id=1, source_target_pairs={{0,3},{1,0},{2,1},{3,2},{4,7},{5,4},{6,5},{7,6},{8,11},{9,8},{10,9... | collective-permute-start | bytes 1253384 | tf_op jit(solution)/shard_map/ppermute | solution.py:386
  54.4 24.8 %collective-permute-start.1 = (bf16[17,96,128]{2,1,0:T(8,128)(2,1)S(1)}, bf16[17,96,128]{2,1,0:T(8,128)(2,1)S(1)}, u32[]{:S(2)}, u32[]{:S(2)}) collective-permute-start(bf16[17,96,128]{2,1,0:T(8,128)(2,1)S(1)} %copy-done.4), channel_id=1, source_target_pairs={{0,1},{1,2},{2,3},{3,0},{4,5},{5,6},{6,7},{7,4},{8,9},{9,10},{10,1... | collective-permute-start | bytes 1253384 | tf_op jit(solution)/shard_map/ppermute | solution.py:386
  54.4 34.1 %collective-permute-start.3 = (bf16[17,96,128]{2,1,0:T(8,128)(2,1)S(1)}, bf16[17,96,128]{2,1,0:T(8,128)(2,1)S(1)}, u32[]{:S(2)}, u32[]{:S(2)}) collective-permute-start(bf16[17,96,128]{2,1,0:T(8,128)(2,1)S(1)} %copy-done.3), channel_id=1, source_target_pairs={{0,2},{1,3},{2,0},{3,1},{4,6},{5,7},{6,4},{7,5},{8,10},{9,11},{10,... | collective-permute-start | bytes 1253384 | tf_op jit(solution)/shard_map/ppermute | solution.py:386
  79.2 9.4 %slice-start.2 = ((bf16[17,96,128]{2,1,0:T(8,128)(2,1)}), bf16[7,96,128]{2,1,0:T(8,128)(2,1)S(1)}, s32[]{:S(2)}) async-start(bf16[17,96,128]{2,1,0:T(8,128)(2,1)} %pack.8.refs_0_), calls=%async_computation.2 | async-start | bytes 344064 | tf_op jit(solution)/shard_map/slice | solution.py:404
  88.6 17.8 %copy-start.1 = (bf16[17,96,128]{2,1,0:T(8,128)(2,1)S(1)}, bf16[17,96,128]{2,1,0:T(8,128)(2,1)}, u32[]{:S(2)}) copy-start(bf16[17,96,128]{2,1,0:T(8,128)(2,1)} %pack.8.refs_0_) | copy-start | bytes 1253380
  88.7 14.1 %collective-permute-start.9 = (bf16[7,384,128]{2,1,0:T(8,128)(2,1)S(1)}, bf16[7,384,128]{2,1,0:T(8,128)(2,1)S(1)}, u32[]{:S(2)}, u32[]{:S(2)}) collective-permute-start(bf16[7,384,128]{2,1,0:T(8,128)(2,1)S(1)} %pad_maximum_fusion.2), channel_id=1, source_target_pairs={{4,0},{8,4},{12,8},{16,12},{20,16},{24,20},{28,24},{0,28},{5,1},{9... | collective-permute-start | bytes 2064392 | tf_op jit(solution)/shard_map/ppermute | solution.py:412
  89.5 17.0 %collective-permute-start.8 = (bf16[7,384,128]{2,1,0:T(8,128)(2,1)S(1)}, bf16[7,384,128]{2,1,0:T(8,128)(2,1)S(1)}, u32[]{:S(2)}, u32[]{:S(2)}) collective-permute-start(bf16[7,384,128]{2,1,0:T(8,128)(2,1)S(1)} %maximum_maximum_fusion), channel_id=1, source_target_pairs={{0,4},{4,8},{8,12},{12,16},{16,20},{20,24},{24,28},{28,0},{1,5},{5... | collective-permute-start | bytes 2064392 | tf_op jit(solution)/shard_map/ppermute | solution.py:411
  89.6 36.2 %collective-permute-start.13 = (bf16[16,96,128]{2,1,0:T(8,128)(2,1)S(1)}, bf16[16,96,128]{2,1,0:T(8,128)(2,1)S(1)}, u32[]{:S(2)}, u32[]{:S(2)}) collective-permute-start(bf16[16,96,128]{2,1,0:T(8,128)(2,1)S(1)} %get-tuple-element.27), channel_id=1, source_target_pairs={{0,3},{1,0},{2,1},{3,2},{4,7},{5,4},{6,5},{7,6},{8,11},{9,8},{10,9... | collective-permute-start | bytes 1179656 | tf_op jit(solution)/shard_map/ppermute | solution.py:386
  92.3 34.1 %collective-permute-start.14 = (bf16[16,96,128]{2,1,0:T(8,128)(2,1)S(1)}, bf16[16,96,128]{2,1,0:T(8,128)(2,1)S(1)}, u32[]{:S(2)}, u32[]{:S(2)}) collective-permute-start(bf16[16,96,128]{2,1,0:T(8,128)(2,1)S(1)} %get-tuple-element.28), channel_id=1, source_target_pairs={{0,2},{1,3},{2,0},{3,1},{4,6},{5,7},{6,4},{7,5},{8,10},{9,11},{10,... | collective-permute-start | bytes 1179656 | tf_op jit(solution)/shard_map/ppermute | solution.py:386
  92.3 34.1 %collective-permute-start.15 = (bf16[16,96,128]{2,1,0:T(8,128)(2,1)S(1)}, bf16[16,96,128]{2,1,0:T(8,128)(2,1)S(1)}, u32[]{:S(2)}, u32[]{:S(2)}) collective-permute-start(bf16[16,96,128]{2,1,0:T(8,128)(2,1)S(1)} %get-tuple-element.29), channel_id=1, source_target_pairs={{0,1},{1,2},{2,3},{3,0},{4,5},{5,6},{6,7},{7,4},{8,9},{9,10},{10,1... | collective-permute-start | bytes 1179656 | tf_op jit(solution)/shard_map/ppermute | solution.py:386
  123.0 12.3 %collective-permute-start.12 = (bf16[16,96,128]{2,1,0:T(8,128)(2,1)S(1)}, bf16[16,96,128]{2,1,0:T(8,128)(2,1)S(1)}, u32[]{:S(2)}, u32[]{:S(2)}) collective-permute-start(bf16[16,96,128]{2,1,0:T(8,128)(2,1)S(1)} %get-tuple-element.38), channel_id=1, source_target_pairs={{0,3},{1,0},{2,1},{3,2},{4,7},{5,4},{6,5},{7,6},{8,11},{9,8},{10,9... | collective-permute-start | bytes 1179656 | tf_op jit(solution)/shard_map/ppermute | solution.py:386
  125.7 34.0 %collective-permute-start.11 = (bf16[16,96,128]{2,1,0:T(8,128)(2,1)S(1)}, bf16[16,96,128]{2,1,0:T(8,128)(2,1)S(1)}, u32[]{:S(2)}, u32[]{:S(2)}) collective-permute-start(bf16[16,96,128]{2,1,0:T(8,128)(2,1)S(1)} %get-tuple-element.36), channel_id=1, source_target_pairs={{0,2},{1,3},{2,0},{3,1},{4,6},{5,7},{6,4},{7,5},{8,10},{9,11},{10,... | collective-permute-start | bytes 1179656 | tf_op jit(solution)/shard_map/ppermute | solution.py:386
  125.8 35.2 %collective-permute-start.10 = (bf16[16,96,128]{2,1,0:T(8,128)(2,1)S(1)}, bf16[16,96,128]{2,1,0:T(8,128)(2,1)S(1)}, u32[]{:S(2)}, u32[]{:S(2)}) collective-permute-start(bf16[16,96,128]{2,1,0:T(8,128)(2,1)S(1)} %get-tuple-element.35), channel_id=1, source_target_pairs={{0,1},{1,2},{2,3},{3,0},{4,5},{5,6},{6,7},{7,4},{8,9},{9,10},{10,1... | collective-permute-start | bytes 1179656 | tf_op jit(solution)/shard_map/ppermute | solution.py:386
  (5 other events, 6.6 us)
